TPU v7x, 512 devices: a whole 4x4x16 slice. The times are simulated.
512 devices in a mesh: row: 16 (over y, z_hi), col: 32 (over z_lo, x, core).
Axes of the slice: x: 4, y: 4, z: 16 (z_hi: 4, z_lo: 4; z = z_hi * 4 + z_lo), core: 2. Of those that a mesh axis runs over, the one named last changes fastest.
Arguments:
- features: bfloat16 [65536, 256], P(('col', 'row')), may hold values from -6 to 6
- weight: bfloat16 [256, 256], replicated, may hold values from -0.375 to 0.375
- tiles: bfloat16 [16, 32, 96, 128, 128], P('row', 'col'), may hold values from -0.09375 to 0.09375
- coords: int32 [16, 32, 96, 2], P('row', 'col'), may hold values from 0 to 31, as said below
- counts: int32 [16, 32], P('row', 'col'), may hold values from 12 to 96, as said below
- cotangent: bfloat16 [65536, 256], P(('row', 'col')), may hold values from -6 to 6
Outputs:
- output: bfloat16 [65536, 256], P(('row', 'col'))
- grad_features: bfloat16 [65536, 256], P(('col', 'row'))
- grad_weight: float32 [256, 256], replicated
Inputs may be any that keep to these rules, and one draw needn't show every extreme that they name: `coords`: within one device the slots name distinct tile positions; the first entry is below 32, the second below 16. `counts`: some device has all 96 slots live in every draw.
All inputs are finite; a program needn't handle non-finite values.
Results may differ from a plain program's by a relative error of at most 0.017.
Values may be sent and summed in bfloat16 or wider, within the bound.
A program may use at most 64 MiB of HBM per device.

v0:
```python
import math

import jax
import jax.numpy as jnp
from jax import lax
from jax.sharding import PartitionSpec as P


def silu_slope(hidden):
    sig = jax.nn.sigmoid(hidden)
    return sig * (1.0 + hidden * (1.0 - sig))


def tile_products(
    my_tiles, my_coords, live_count, source, which_source, which_target, target_len, transpose
):
    slot_total = my_tiles.shape[0]
    tile_size = my_tiles.shape[1]
    width = source.shape[2]
    block_size = math.gcd(slot_total, 16)
    block_total = slot_total // block_size
    target_ids = jnp.arange(target_len, dtype=jnp.int32)
    form = "sji,sjh->sih" if transpose else "sij,sjh->sih"

    def add_block(step, total):
        begin = step * block_size
        block_tiles = lax.dynamic_slice_in_dim(my_tiles, begin, block_size, 0)
        block_coords = lax.dynamic_slice_in_dim(my_coords, begin, block_size, 0)
        live = begin + jnp.arange(block_size, dtype=jnp.int32) < live_count
        picked = source[block_coords[:, which_source]]
        prod = jnp.einsum(form, block_tiles, picked, preferred_element_type=jnp.float32)
        onehot = (
            (block_coords[:, which_target][:, None] == target_ids[None, :]) & live[:, None]
        ).astype(jnp.float32)
        return total + jnp.einsum("sr,sih->rih", onehot, prod)

    start = jnp.zeros((target_len, tile_size, width), jnp.float32)
    return lax.fori_loop(0, block_total, add_block, start)


def body(features, weight, tiles, coords, counts, cotangent):
    my_tiles = tiles[0, 0]
    my_coords = coords[0, 0]
    live_count = counts[0, 0]
    tile_size = my_tiles.shape[1]
    width = weight.shape[1]
    node_rows = features.shape[0]
    tile_cols = node_rows * lax.axis_size("row") // tile_size
    tile_rows = node_rows * lax.axis_size("col") // tile_size
    gathered = lax.all_gather(features, "row", axis=0, tiled=True)
    panel = jnp.dot(gathered, weight, preferred_element_type=jnp.float32).astype(jnp.bfloat16)
    panel_tiles = panel.reshape(tile_cols, tile_size, width)
    partial_sum = tile_products(
        my_tiles, my_coords, live_count, panel_tiles, 1, 0, tile_rows, False
    )
    own_hidden = lax.psum_scatter(
        partial_sum.reshape(tile_rows * tile_size, width), "col", scatter_dimension=0, tiled=True
    )
    output = jax.nn.silu(own_hidden).astype(jnp.bfloat16)
    grad_own = (cotangent.astype(jnp.float32) * silu_slope(own_hidden)).astype(jnp.bfloat16)
    grad_slab = lax.all_gather(grad_own, "col", axis=0, tiled=True)
    grad_tiles = grad_slab.reshape(tile_rows, tile_size, width)
    back_partial = tile_products(my_tiles, my_coords, live_count, grad_tiles, 0, 1, tile_cols, True)
    grad_projected = lax.psum_scatter(
        back_partial.reshape(tile_cols * tile_size, width), "row", scatter_dimension=0, tiled=True
    ).astype(jnp.bfloat16)
    grad_features = jnp.dot(grad_projected, weight.T, preferred_element_type=jnp.float32).astype(
        jnp.bfloat16
    )
    weight_term = jnp.dot(features.T, grad_projected, preferred_element_type=jnp.float32)
    grad_weight = lax.psum(weight_term, ("row", "col"))
    return (output, grad_features, grad_weight)


def solution(mesh):
    placed = (
        P(("col", "row"), None),
        P(),
        P("row", "col", None, None, None),
        P("row", "col", None, None),
        P("row", "col"),
        P(("row", "col"), None),
    )
    return jax.shard_map(
        body,
        mesh=mesh,
        in_specs=placed,
        out_specs=(P(("row", "col"), None), P(("col", "row"), None), P()),
        check_vma=False,
    )
```

profile of v0, /device:TPU:6, one launch (start us, length us, event | category | flops | bytes accessed | tf_op | source)
XLA Modules:
  0.0 1010.1 jit_solution(9324999141770844763)
XLA Ops:
  8.0 84.9 %all-gather.3.cloned.1.call-done = bf16[2048,256]{1,0:T(8,128)(2,1)} async-done(((bf16[128,256]{1,0:T(8,128)(2,1)}), bf16[2048,256]{1,0:T(8,128)(2,1)}) %all-gather.3.cloned.1.call-update) | async-done | bytes 1048592 | tf_op jit(solution)/shard_map/all_gather | solution.py:50
  92.9 1.7 convolution_convert_fusion
  94.6 50.4 %while.28 = (s32[]{:T(128)}, f32[32,128,256]{2,0,1:T(8,128)}, s32[96,2]{0,1:T(2,128)}, s32[]{:T(128)}, bf16[96,128,128]{2,1,0:T(8,128)(2,1)}, /*index=5*/bf16[16...) while((s32[]{:T(128)}, f32[32,128,256]{2,0,1:T(8,128)}, ...), condition=%wide.region_1.0_spmd.clone, body=%wide.region_0.0_spmd.clone.sunk | while | flops 169871440 | bytes 14160781 | solution.py:38
  94.6 0.8 constant_dynamic-slice_fusion.4
  96.0 1.5 fusion.49
  98.1 3.1 select_add_fusion.4
  101.2 0.7 constant_dynamic-slice_fusion.4
  102.6 1.5 fusion.49
  104.7 5.2 select_add_fusion.4
  109.9 0.7 constant_dynamic-slice_fusion.4
  111.3 1.5 fusion.49
  113.5 5.2 select_add_fusion.4
  118.7 0.7 constant_dynamic-slice_fusion.4
  120.1 1.5 fusion.49
  122.2 5.2 select_add_fusion.4
  128.9 1.5 fusion.49
  131.0 5.2 select_add_fusion.4
  137.6 1.5 fusion.49
  139.7 5.2 select_add_fusion.4
  145.0 6.6 copy.11
  151.6 133.3 %reduce-scatter.3.cloned.1.call-done = f32[128,256]{1,0:T(8,128)} async-done(((f32[4096,256]{1,0:T(8,128)}), f32[128,256]{1,0:T(8,128)}) %reduce-scatter.3.cloned.1.call-update) | async-done | bytes 131088 | tf_op jit(solution)/shard_map/reduce_scatter | solution.py:56
  285.0 1.6 multiply_convert_fusion
  286.7 79.1 %all-gather.5.cloned.1.call-done = bf16[4096,256]{1,0:T(8,128)(2,1)} async-done(((bf16[128,256]{1,0:T(8,128)(2,1)}), bf16[4096,256]{1,0:T(8,128)(2,1)}) %all-gather.5.cloned.1.call-update) | async-done | bytes 2097168 | tf_op jit(solution)/shard_map/all_gather | solution.py:61
  365.8 47.5 %while.29 = (s32[]{:T(128)}, f32[16,128,256]{2,0,1:T(8,128)}, s32[96,2]{0,1:T(2,128)S(1)}, s32[]{:T(128)}, bf16[96,128,128]{2,1,0:T(8,128)(2,1)}, /*index=5*/bf1...) while((s32[]{:T(128)}, f32[16,128,256]{2,0,1:T(8,128)}, ...), condition=%wide.region_4.5_spmd.clone, body=%wide.region_3.4_spmd.clone.sunk | while | flops 152045136 | bytes 9966477 | solution.py:38
  365.9 2.2 gather_fusion.1
  368.1 1.5 fusion.54
  370.3 2.1 select_add_fusion.5
  372.5 2.2 gather_fusion.1
  374.7 1.5 fusion.54
  376.9 3.7 select_add_fusion.5
  380.7 2.2 gather_fusion.1
  382.9 1.5 fusion.54
  385.1 3.7 select_add_fusion.5
  388.9 2.2 gather_fusion.1
  391.1 1.5 fusion.54
  393.3 3.7 select_add_fusion.5
  397.1 2.2 gather_fusion.1
  399.3 1.5 fusion.54
  401.5 3.7 select_add_fusion.5
  405.2 2.2 gather_fusion.1
  407.5 1.5 fusion.54
  409.7 3.7 select_add_fusion.5
  413.3 4.2 copy.12
  417.6 126.0 %reduce-scatter.5.cloned.1.call-done = f32[128,256]{1,0:T(8,128)} async-done(((f32[2048,256]{1,0:T(8,128)}), f32[128,256]{1,0:T(8,128)}) %reduce-scatter.5.cloned.1.call-update) | async-done | bytes 131088 | tf_op jit(solution)/shard_map/reduce_scatter | solution.py:64
  543.6 1.8 convolution_bitcast_fusion
  545.4 1.7 convolution_convert_fusion.1
  547.2 454.6 %all-reduce.2.cloned.1.call-done = f32[256,256]{0,1:T(8,128)} async-done(((f32[256,256]{0,1:T(8,128)}), f32[256,256]{0,1:T(8,128)}) %all-reduce.2.cloned.1.call-update) | async-done | bytes 262160 | tf_op jit(solution)/shard_map/psum | solution.py:71
  1001.7 1.8 copy.13
  (70 shorter events, 14.6 us)
Async XLA Ops:
  7.2 85.7 %copy-start = (bf16[256,256]{1,0:T(8,128)(2,1)S(1)}, bf16[256,256]{1,0:T(8,128)(2,1)}, u32[]{:S(2)}) copy-start(bf16[256,256]{1,0:T(8,128)(2,1)} %param.11) | copy-start | bytes 393220
  7.2 85.7 %all-gather.3.cloned.1.call-start = ((), (), s32[]{:S(2)}) async-start(), calls=%async_computation.2 | async-start | bytes 1114112 | tf_op jit(solution)/shard_map/all_gather | solution.py:50
  7.9 277.1 %reduce-scatter.3.cloned.1.call-start = ((), (), s32[]{:S(2)}) async-start(), calls=%async_computation.3 | async-start | bytes 4325376 | tf_op jit(solution)/shard_map/reduce_scatter | solution.py:56
  151.6 133.4 %copy-start.3 = (bf16[128,256]{1,0:T(8,128)(2,1)S(1)}, bf16[128,256]{1,0:T(8,128)(2,1)}, u32[]{:S(2)}) copy-start(bf16[128,256]{1,0:T(8,128)(2,1)} %param.15) | copy-start | bytes 196612
  151.6 214.2 %copy-start.2 = (s32[96,2]{0,1:T(2,128)S(1)}, s32[96,2]{0,1:T(2,128)}, u32[]{:S(2)}) copy-start(s32[96,2]{0,1:T(2,128)} %get-tuple-element.498) | copy-start | bytes 2308
  151.6 214.2 %all-gather.5.cloned.1.call-start = ((), (), s32[]{:S(2)}) async-start(), calls=%async_computation.4 | async-start | bytes 2162688 | tf_op jit(solution)/shard_map/all_gather | solution.py:61
  286.6 257.0 %reduce-scatter.5.cloned.1.call-start = ((), (), s32[]{:S(2)}) async-start(), calls=%async_computation.5 | async-start | bytes 2228224 | tf_op jit(solution)/shard_map/reduce_scatter | solution.py:64
  413.3 130.3 %copy-start.1 = (bf16[128,256]{1,0:T(8,128)(2,1)S(1)}, bf16[128,256]{1,0:T(8,128)(2,1)}, u32[]{:S(2)}) copy-start(bf16[128,256]{1,0:T(8,128)(2,1)} %param.10) | copy-start | bytes 196612
  417.5 584.2 %all-reduce.2.cloned.1.call-start = ((), (), s32[]{:S(2)}) async-start(), calls=%async_computation.6 | async-start | bytes 524288 | tf_op jit(solution)/shard_map/psum | solution.py:71
Sparse Core Ops, SparseCore 0:
  11.0 81.8 all-gather.2
  151.7 133.2 reduce-scatter.2
  287.7 78.0 all-gather.4
  417.7 125.8 reduce-scatter.4
  550.4 451.3 all-reduce.1
where the time goes:
time: 1010 us
  waiting for transfers between devices  879 us (87%)
  matrix products  73 us (7%)
  local copies, waits for them, and re-layouts  34.4 us (3%)
  between operations  13.8 us (1%)
    psum x1, waiting for transfers between devices, body(): grad_weight = lax.psum(weight_term, ('row', 'col'))  455 us
    reduce_scatter x1, waiting for transfers between devices, body(): lax.psum_scatter(partial_sum.reshape(tile_rows * tile_size, width), 'col'...  133 us
    reduce_scatter x1, waiting for transfers between devices, body(): lax.psum_scatter(back_partial.reshape(tile_cols * tile_size, width), 'row...  126 us
    all_gather x1, waiting for transfers between devices, body(): gathered = lax.all_gather(features, 'row', axis=0, tiled=True)  84.9 us
    all_gather x1, waiting for transfers between devices, body(): grad_slab = lax.all_gather(grad_own, 'col', axis=0, tiled=True)  79.1 us
    dot_general x12, matrix products, add_block(): return total + jnp.einsum('sr,sih->rih', onehot, prod)  49.8 us
  transfers between devices with their start and end apart: 5, of which 5 were waited for; matrix products, arithmetic and copies ran while one was open for 0% of the time, Pallas kernels for 0%

commit v1 on v0

v1 whole, which is shorter than its diff:
```python
import functools

import jax
import jax.numpy as jnp
from jax import lax
from jax.experimental import pallas as pl
from jax.experimental.pallas import tpu as pltpu
from jax.sharding import PartitionSpec as P

F32 = jnp.float32
BF16 = jnp.bfloat16
MESH = pl.DeviceIdType.MESH
TILE = 128
HID = 256
TROWS = 32
TCOLS = 16
SLOTS = 96
GROUP = 16
UNROLL = 4
VMEM_LIMIT = 28 * 2**20
LOW = slice(0, 64)
HIGH = slice(64, 128)


def flip1(v):
    return v + 1 - 2 * lax.rem(v, 2)


def flip2(v):
    return lax.rem(v + 2, 4)


def flip3(v):
    return 3 - v


FLIPS = {0: lambda v: v, 1: flip1, 2: flip2, 3: flip3}


class Place:
    def __init__(self):
        row = lax.axis_index("row")
        col = lax.axis_index("col")
        self.y = lax.div(row, 4)
        self.zh = lax.rem(row, 4)
        self.zl = lax.div(col, 8)
        self.x = lax.rem(lax.div(col, 2), 4)
        self.core = lax.rem(col, 2)

    def peer(self, y=0, zh=0, zl=0, x=0, core=0):
        row = FLIPS[y](self.y) * 4 + FLIPS[zh](self.zh)
        col = FLIPS[zl](self.zl) * 8 + FLIPS[x](self.x) * 2 + FLIPS[core](self.core)
        return (row, col)


class Net:
    def __init__(self, send_sems, recv_sems):
        self.send_sems = send_sems
        self.recv_sems = recv_sems
        self.started = []

    def send(self, src, dst, device):
        i = len(self.started)
        copy = pltpu.make_async_remote_copy(
            src_ref=src,
            dst_ref=dst,
            send_sem=self.send_sems.at[i],
            recv_sem=self.recv_sems.at[i],
            device_id=device,
            device_id_type=MESH,
        )
        copy.start()
        self.started.append(copy)
        return copy

    def finish(self):
        for copy in self.started:
            copy.wait_send()


def greet(peers):
    barrier = pltpu.get_barrier_semaphore()
    for peer in peers:
        pl.semaphore_signal(barrier, inc=1, device_id=peer, device_id_type=MESH)
    pl.semaphore_wait(barrier, len(peers))


def add(*values):
    total = values[0].astype(F32)
    for value in values[1:]:
        total = total + value.astype(F32)
    return total.astype(BF16)


def ring_gather(net, at, near, far):
    copies = {}

    def first():
        copies["n"] = net.send(at(0, None), at(1, None), near)
        copies["f"] = net.send(at(0, None), at(3, None), far)

    def second():
        copies["n"].wait_recv()
        copies["nf"] = net.send(at(1, LOW), at(2, LOW), far)
        copies["f"].wait_recv()
        copies["fn"] = net.send(at(3, HIGH), at(2, HIGH), near)

    def third():
        copies["nf"].wait_recv()
        copies["fn"].wait_recv()

    return first, second, third


def ring_scatter(net, at, landing, near, far):
    copies = {}

    def first():
        copies["t1"] = net.send(at(2, LOW), landing.at[2, LOW], near)
        copies["t3"] = net.send(at(2, HIGH), landing.at[2, HIGH], far)
        copies["n0"] = net.send(at(1, LOW), landing.at[0, LOW], near)
        copies["f1"] = net.send(at(3, HIGH), landing.at[1, HIGH], far)

    def second():
        copies["t1"].wait_recv()
        share = at(3, LOW)
        share[...] = add(share[...], landing[2, LOW])
        copies["f0"] = net.send(share, landing.at[1, LOW], far)
        copies["t3"].wait_recv()
        share = at(1, HIGH)
        share[...] = add(share[...], landing[2, HIGH])
        copies["n1"] = net.send(share, landing.at[0, HIGH], near)

    def third():
        for name in ("n0", "f1", "f0", "n1"):
            copies[name].wait_recv()

    return first, second, third


def gather_kernel(features, weight, panel, send_sems, recv_sems):
    place = Place()
    net = Net(send_sems, recv_sems)
    z_near, z_far = place.peer(zh=1), place.peer(zh=3)
    y_near, y_far = place.peer(y=1), place.peer(y=3)
    panel[0, 0] = jnp.dot(features[...], weight[...], preferred_element_type=F32).astype(BF16)
    greet((z_near, z_far, y_near, y_far))

    def at_z(i, rows):
        return panel.at[0, i] if rows is None else panel.at[0, i, rows]

    def at_y(k):
        return lambda i, rows: panel.at[i, k] if rows is None else panel.at[i, k, rows]

    z1, z2, z3 = ring_gather(net, at_z, z_near, z_far)
    rings = [ring_gather(net, at_y(k), y_near, y_far) for k in range(4)]
    z1()
    rings[0][0]()
    rings[0][1]()
    z2()
    rings[1][0]()
    rings[3][0]()
    rings[1][1]()
    rings[3][1]()
    z3()
    rings[2][0]()
    rings[2][1]()
    for k in (0, 1, 3, 2):
        rings[k][2]()
    net.finish()


def products_kernel(back, enc, count, tiles, panel, out, held, acc, sems):
    live = count[0, 0]
    groups = SLOTS // GROUP
    targets = TCOLS if back else TROWS

    def fetch(g):
        part = pl.ds(g * GROUP, GROUP)
        return pltpu.make_async_copy(tiles.at[part], held.at[part], sems.at[g])

    for g in range(groups):
        @pl.when(g * GROUP < live)
        def _():
            fetch(g).start()

    def clear(t, carry):
        acc[t] = jnp.zeros((TILE, HID), F32)
        return carry

    lax.fori_loop(0, targets, clear, 0)

    def product(slot):
        code = enc[slot]
        first, second = lax.shift_right_logical(code, 4), lax.bitwise_and(code, 15)
        target, source = (second, first) if back else (first, second)
        target = jnp.where(slot < live, target, targets)
        dims = (((0,), (0,)), ((), ())) if back else (((1,), (0,)), ((), ()))
        value = lax.dot_general(held[slot], panel[source], dims, preferred_element_type=F32)
        return target, value

    for g in range(groups):
        @pl.when(g * GROUP < live)
        def _():
            fetch(g).wait()

            def step(i, carry):
                base = g * GROUP + i * UNROLL
                done = [product(base + u) for u in range(UNROLL)]
                for target, value in done:
                    acc[target] += value
                return carry

            steps = lax.min(lax.div(live - g * GROUP + UNROLL - 1, UNROLL), GROUP // UNROLL)
            lax.fori_loop(0, steps, step, 0)

    def pack(t, carry):
        out[t] = acc[t].astype(BF16)
        return carry

    lax.fori_loop(0, targets, pack, 0)


def middle_kernel(
    partial, cotangent, output, grads, from_core, from_x, total, from_z, send_sems, recv_sems
):
    place = Place()
    net = Net(send_sems, recv_sems)
    other = place.peer(core=1)
    near, far = place.peer(x=1), place.peer(x=3)
    along = {k: place.peer(zl=k) for k in (1, 2, 3)}
    greet((other, near, far, along[1], along[2], along[3]))
    order = (3, 2, 1, 0)

    core_copies = {
        k: net.send(partial.at[k, :, 1], from_core.at[k], other) for k in order
    }

    def at_x(k):
        return lambda i, rows: from_core.at[k, i, rows]

    rings = {k: ring_scatter(net, at_x(k), from_x.at[k], near, far) for k in order}
    z_copies = {}

    def start(k):
        core_copies[k].wait_recv()
        for i in (2, 1, 3):
            from_core[k, i] = add(from_core[k, i], partial[k, i, 0])
        rings[k][0]()

    def close(k):
        rings[k][2]()
        parts = (partial[k, 0, 0], from_core[k, 0], from_x[k, 0], from_x[k, 1])
        if k:
            total[k] = add(*parts)
            z_copies[k] = net.send(total.at[k], from_z.at[k], along[k])
            return None
        return sum(part.astype(F32) for part in parts)

    start(3)
    start(2)
    rings[3][1]()
    start(1)
    rings[2][1]()
    close(3)
    start(0)
    rings[1][1]()
    close(2)
    rings[0][1]()
    close(1)
    hidden = close(0)
    for k in (3, 2, 1):
        z_copies[k].wait_recv()
        hidden = hidden + from_z[k].astype(F32)
    sig = jax.nn.sigmoid(hidden)
    slope = sig * (1.0 + hidden * (1.0 - sig))
    grads[0, 0, 0] = (cotangent[...].astype(F32) * slope).astype(BF16)

    out_copies = {k: net.send(grads.at[0, 0, 0], grads.at[k, 0, 0], along[k]) for k in (1, 2, 3)}

    def at_g(k):
        return lambda i, rows: grads.at[k, i, 0] if rows is None else grads.at[k, i, 0, rows]

    rounds = {k: ring_gather(net, at_g(k), near, far) for k in range(4)}
    rounds[0][0]()
    output[...] = (hidden * sig).astype(BF16)
    last = {}

    def swap(k):
        rounds[k][2]()
        last[k] = net.send(grads.at[k, :, 0], grads.at[k, :, 1], other)

    out_copies[1].wait_recv()
    rounds[1][0]()
    rounds[0][1]()
    out_copies[2].wait_recv()
    rounds[2][0]()
    rounds[1][1]()
    swap(0)
    out_copies[3].wait_recv()
    rounds[3][0]()
    rounds[2][1]()
    swap(1)
    rounds[3][1]()
    swap(2)
    swap(3)
    for k in range(4):
        last[k].wait_recv()
    net.finish()


def final_kernel(
    partial, features, weight, grad_features, grad_weight,
    from_y, total, from_zh, shares, got8, sum8, got4, got16, all4, all8, send_sems, recv_sems,
):
    place = Place()
    net = Net(send_sems, recv_sems)
    y_peers = {i: place.peer(y=i) for i in (1, 2, 3)}
    z_pairs = [(h, l) for h in range(4) for l in range(4) if h or l]
    z_peers = {pair: place.peer(zh=pair[0], zl=pair[1]) for pair in z_pairs}
    x_pairs = [(i, j) for i in range(4) for j in range(2) if i or j]
    x_peers = {pair: place.peer(x=pair[0], core=pair[1]) for pair in x_pairs}
    greet(tuple(y_peers.values()) + tuple(z_peers.values()) + tuple(x_peers.values()))
    order = (2, 1, 3, 0)

    def at_y(k):
        return lambda i, rows: partial.at[i, k, rows]

    rings = {k: ring_scatter(net, at_y(k), from_y.at[k], y_peers[1], y_peers[3]) for k in order}
    z_near, z_far = z_peers[(1, 0)], z_peers[(3, 0)]

    def close(k):
        rings[k][2]()
        total[k] = add(partial[0, k], from_y[k, 0], from_y[k, 1])

    rings[2][0]()
    rings[1][0]()
    rings[2][1]()
    rings[3][0]()
    rings[1][1]()
    close(2)
    transit1 = net.send(total.at[2, LOW], from_zh.at[2, LOW], z_near)
    transit3 = net.send(total.at[2, HIGH], from_zh.at[2, HIGH], z_far)
    rings[0][0]()
    rings[3][1]()
    close(1)
    near0 = net.send(total.at[1, LOW], from_zh.at[0, LOW], z_near)
    rings[0][1]()
    close(3)
    far1 = net.send(total.at[3, HIGH], from_zh.at[1, HIGH], z_far)
    transit1.wait_recv()
    total[3, LOW] = add(total[3, LOW], from_zh[2, LOW])
    far0 = net.send(total.at[3, LOW], from_zh.at[1, LOW], z_far)
    transit3.wait_recv()
    total[1, HIGH] = add(total[1, HIGH], from_zh[2, HIGH])
    near1 = net.send(total.at[1, HIGH], from_zh.at[0, HIGH], z_near)
    rings[0][2]()
    own = partial[0, 0].astype(F32) + from_y[0, 0].astype(F32) + from_y[0, 1].astype(F32)
    for copy in (near0, far1, far0, near1):
        copy.wait_recv()
    own = own + from_zh[0].astype(F32) + from_zh[1].astype(F32)
    projected = own.astype(BF16)

    term = lax.dot_general(
        features[...], projected, (((0,), (0,)), ((), ())), preferred_element_type=F32
    ).astype(BF16)
    for p in range(8):
        for q in range(4):
            rows = p * 32 + (q // 2) * 16
            lanes = (q % 2) * 128
            shares[p, q] = term[rows:rows + 16, lanes:lanes + 128]

    me8 = place.x * 2 + place.core
    me16 = place.zh * 4 + place.zl
    copies = []
    for n, (i, j) in enumerate(x_pairs):
        there = FLIPS[i](place.x) * 2 + FLIPS[j](place.core)
        copies.append(net.send(shares.at[there], got8.at[n], x_peers[(i, j)]))
    grad_features[...] = lax.dot_general(
        projected, weight[...], (((1,), (1,)), ((), ())), preferred_element_type=F32
    ).astype(BF16)
    sum_own = shares[me8].astype(F32)
    for n, copy in enumerate(copies):
        copy.wait_recv()
        sum_own = sum_own + got8[n].astype(F32)
    sum8[...] = sum_own.astype(BF16)

    copies = [
        net.send(sum8.at[FLIPS[i](place.y)], got4.at[i - 1], y_peers[i]) for i in (1, 2, 3)
    ]
    sum_own = sum8[place.y].astype(F32)
    for i, copy in enumerate(copies):
        copy.wait_recv()
        sum_own = sum_own + got4[i].astype(F32)
    got16[me16] = sum_own.astype(BF16)

    copies = [net.send(got16.at[me16], got16.at[me16], z_peers[pair]) for pair in z_pairs]
    for copy in copies:
        copy.wait_recv()
    sum_all = got16[0].astype(F32)
    for n in range(1, 16):
        sum_all = sum_all + got16[n].astype(F32)
    all4[place.y] = sum_all.astype(BF16)

    copies = [net.send(all4.at[place.y], all4.at[place.y], y_peers[i]) for i in (1, 2, 3)]
    for copy in copies:
        copy.wait_recv()
    all8[me8] = all4[...]
    copies = [net.send(all4, all8.at[me8], x_peers[pair]) for pair in x_pairs]
    for copy in copies:
        copy.wait_recv()
    for p in range(8):
        for q in range(4):
            rows = p * 32 + (q // 2) * 16
            lanes = (q % 2) * 128
            grad_weight[rows:rows + 16, lanes:lanes + 128] = all8[p, q].astype(F32)
    net.finish()


VM = pl.BlockSpec(memory_space=pltpu.VMEM)
SM = pl.BlockSpec(memory_space=pltpu.SMEM)
ANY = pl.BlockSpec(memory_space=pl.ANY)


def shape(*dims, dtype=BF16):
    return jax.ShapeDtypeStruct(dims, dtype)


def comm_params(number):
    return pltpu.CompilerParams(
        collective_id=number, has_side_effects=True, vmem_limit_bytes=VMEM_LIMIT
    )


def links(count):
    return [pltpu.SemaphoreType.DMA((count,)), pltpu.SemaphoreType.DMA((count,))]


def products(back, enc, count, tiles, panel):
    targets = TCOLS if back else TROWS
    return pl.pallas_call(
        functools.partial(products_kernel, back),
        out_shape=shape(targets, TILE, HID),
        in_specs=[SM, SM, ANY, VM],
        out_specs=VM,
        scratch_shapes=[
            pltpu.VMEM((SLOTS, TILE, TILE), BF16),
            pltpu.VMEM((targets + 1, TILE, HID), F32),
            pltpu.SemaphoreType.DMA((SLOTS // GROUP,)),
        ],
        compiler_params=pltpu.CompilerParams(vmem_limit_bytes=VMEM_LIMIT),
        name="back_products" if back else "products",
    )(enc, count, tiles, panel)


def body(features, weight, tiles, coords, counts, cotangent):
    my_coords = coords[0, 0]
    enc = (my_coords[:, 0] ^ lax.axis_index("col")) * 16 + (
        my_coords[:, 1] ^ lax.axis_index("row")
    )
    my_tiles = tiles[0, 0]

    panel = pl.pallas_call(
        gather_kernel,
        out_shape=shape(4, 4, TILE, HID),
        in_specs=[VM, VM],
        out_specs=VM,
        scratch_shapes=links(20),
        compiler_params=comm_params(1),
        name="gather_panel",
    )(features, weight)

    partial = products(False, enc, counts, my_tiles, panel.reshape(TCOLS, TILE, HID))

    output, grads = pl.pallas_call(
        middle_kernel,
        out_shape=(shape(TILE, HID), shape(4, 4, 2, TILE, HID)),
        in_specs=[VM, VM],
        out_specs=(VM, VM),
        scratch_shapes=[
            pltpu.VMEM((4, 4, TILE, HID), BF16),
            pltpu.VMEM((4, 3, TILE, HID), BF16),
            pltpu.VMEM((4, TILE, HID), BF16),
            pltpu.VMEM((4, TILE, HID), BF16),
        ] + links(64),
        compiler_params=comm_params(2),
        name="hidden_and_slope",
    )(partial.reshape(4, 4, 2, TILE, HID), cotangent)

    back = products(True, enc, counts, my_tiles, grads.reshape(TROWS, TILE, HID))

    grad_features, grad_weight = pl.pallas_call(
        final_kernel,
        out_shape=(shape(TILE, HID), shape(HID, HID, dtype=F32)),
        in_specs=[VM, VM, VM],
        out_specs=(VM, VM),
        scratch_shapes=[
            pltpu.VMEM((4, 3, TILE, HID), BF16),
            pltpu.VMEM((4, TILE, HID), BF16),
            pltpu.VMEM((3, TILE, HID), BF16),
            pltpu.VMEM((8, 4, 16, 128), BF16),
            pltpu.VMEM((7, 4, 16, 128), BF16),
            pltpu.VMEM((4, 16, 128), BF16),
            pltpu.VMEM((3, 16, 128), BF16),
            pltpu.VMEM((16, 16, 128), BF16),
            pltpu.VMEM((4, 16, 128), BF16),
            pltpu.VMEM((8, 4, 16, 128), BF16),
        ] + links(68),
        compiler_params=comm_params(3),
        name="gradients",
    )(back.reshape(4, 4, TILE, HID), features, weight)
    return output, grad_features, grad_weight


def solution(mesh):
    placed = (
        P(("col", "row"), None),
        P(),
        P("row", "col", None, None, None),
        P("row", "col", None, None),
        P("row", "col"),
        P(("row", "col"), None),
    )
    return jax.shard_map(
        body,
        mesh=mesh,
        in_specs=placed,
        out_specs=(P(("row", "col"), None), P(("col", "row"), None), P()),
        check_vma=False,
    )
```

time: 1010 us -> 144 us (0.14)
  waiting for transfers between devices: 879 us -> 0 us
  Pallas kernels: 0 us -> 134 us
  matrix products: 73 us -> 0 us
  local copies, waits for them, and re-layouts: 34.4 us -> 5.6 us
  between operations: 13.8 us -> 1.36 us
    psum x1 -> x0, waiting for transfers between devices: 455 us -> none  [body(): grad_weight = lax.psum(weight_term, ('row', 'col'))]
    reduce_scatter x2 -> x0, waiting for transfers between devices: 259 us -> none  [the longest x1 133 us: body(): lax.psum_scatter(partial_sum.reshape(tile_rows * tile_size, width), 'col'...]
    all_gather x2 -> x0, waiting for transfers between devices: 164 us -> none  [the longest x1 84.9 us: body(): gathered = lax.all_gather(features, 'row', axis=0, tiled=True)]
    pallas_call x0 -> x5, Pallas kernels: none -> 134 us  [the longest x1 57 us: body(): pl.pallas_call(final_kernel, out_shape=(shape(TILE, HID), shape(HID, HID,...]
    dot_general x27 -> x0, matrix products: 73 us -> none  [the longest x12 49.8 us: add_block(): return total + jnp.einsum('sr,sih->rih', onehot, prod)]
    gather x12 -> x0, local copies, waits for them, and re-layouts: 16.9 us -> none  [add_block(): picked = source[block_coords[:, which_source]]]
    while x2 -> x0, local copies, waits for them, and re-layouts: 10.8 us -> none  [tile_products(): return lax.fori_loop(0, block_total, add_block, start)]
  transfers between devices with their start and end apart: 5 -> 0, of which waited for: 5 -> 0; matrix products, arithmetic and copies ran while one was open for 0% -> 0% of each run, Pallas kernels for 0% -> 0%
where the time goes in v1:
time: 144 us; the launch traced here: 141 us
  Pallas kernels  134 us (93%)
  local copies, waits for them, and re-layouts  5.6 us (4%)
    pallas_call x1, Pallas kernels, body(): pl.pallas_call(final_kernel, out_shape=(shape(TILE, HID), shape(HID, HID,...  57 us
    pallas_call x1, Pallas kernels, body(): pl.pallas_call(middle_kernel, out_shape=(shape(TILE, HID), shape(4, 4, 2,...  35.8 us
    pallas_call x1, Pallas kernels, body(): pl.pallas_call(gather_kernel, out_shape=shape(4, 4, TILE, HID), in_specs=...  34.5 us
    pallas_call x2, Pallas kernels, products(): pl.pallas_call(functools.partial(products_kernel, back), out_shape=shape(...  6.33 us
    unnamed x15, local copies, waits for them, and re-layouts  5.6 us

profile of v1, /device:TPU:6, one launch (start us, length us, event | category | flops | bytes accessed | tf_op | source)
XLA Modules:
  0.0 141.5 jit_solution(5420814855851572344)
XLA Ops:
  1.3 0.8 add_bitcast_fusion.enc
  2.0 0.0 copy-start.2
  2.0 0.9 copy-done.2
  2.9 0.0 copy-start.3
  2.9 0.8 copy-done.3
  3.8 34.5 %gather_panel.1 = bf16[4,4,128,256]{3,2,1,0:T(8,128)(2,1)S(1)} custom-call(bf16[128,256]{1,0:T(8,128)(2,1)S(1)} %copy-done.3, bf16[256,256]{1,0:T(8,128)(2,1)S(1)} %copy-done.2), custom_call_target="tpu_custom_call" | custom-call | tf_op jit(solution)/shard_map/gather_panel/pallas_call | solution.py:463
  38.3 0.0 copy-start
  38.3 1.9 %copy-done = bf16[1,1,96,128,128]{4,3,2,1,0:T(8,128)(2,1)S(1)} copy-done((bf16[1,1,96,128,128]{4,3,2,1,0:T(8,128)(2,1)S(1)}, bf16[1,1,96,128,128]{4,3,2,1,0:T(8,128)(2,1)}, u32[]{:S(2)}) %copy-start) | copy-done | bytes 3145752
  40.2 0.0 copy-start.5
  40.2 0.0 copy-start.1
  40.2 3.2 %products.1 = bf16[32,128,256]{2,1,0:T(8,128)(2,1)S(1)} custom-call(s32[96]{0:T(128)S(1)} %add_bitcast_fusion.enc, s32[1,1]{1,0:T(1,128)S(6)} %copy.12.count, bf16[96,128,128]{2,1,0:T(8,128)(2,1)S(1)} %bitcast.8, bf16[16,128,256]{2,1,0:T(8,128)(2,1)S(1)} %bitcast.12), custom_call_target="tpu_custom_call" | custom-call | tf_op jit(solution)/shard_map/products/pallas_call | solution.py:441
  43.4 0.0 copy-done.5
  43.4 35.8 %hidden_and_slope.1 = (bf16[128,256]{1,0:T(8,128)(2,1)S(1)}, bf16[4,4,2,128,256]{4,3,2,1,0:T(8,128)(2,1)S(1)}) custom-call(bf16[4,4,2,128,256]{4,3,2,1,0:T(8,128)(2,1)S(1)} %bitcast.10, bf16[128,256]{1,0:T(8,128)(2,1)S(1)} %copy-done.5), custom_call_target="tpu_custom_call" | custom-call | tf_op jit(solution)/shard_map/hidden_and_slope/pallas_call | solution.py:475
  79.2 0.0 copy-done.1
  79.3 0.0 copy-start.4
  79.3 3.1 %back_products.1 = bf16[16,128,256]{2,1,0:T(8,128)(2,1)S(1)} custom-call(s32[96]{0:T(128)S(1)} %add_bitcast_fusion.enc, s32[1,1]{1,0:T(1,128)S(6)} %copy.12.count, bf16[96,128,128]{2,1,0:T(8,128)(2,1)S(1)} %bitcast.9, bf16[32,128,256]{2,1,0:T(8,128)(2,1)S(1)} %bitcast.13), custom_call_target="tpu_custom_call" | custom-call | tf_op jit(solution)/shard_map/back_products/pallas_call | solution.py:441
  82.4 0.0 copy-done.4
  82.4 57.0 %gradients.1 = (bf16[128,256]{1,0:T(8,128)(2,1)S(1)}, f32[256,256]{1,0:T(8,128)S(1)}) custom-call(bf16[4,4,128,256]{3,2,1,0:T(8,128)(2,1)S(1)} %bitcast.11, bf16[128,256]{1,0:T(8,128)(2,1)S(1)} %copy-done.4, bf16[256,256]{1,0:T(8,128)(2,1)S(1)} %copy-done.2), custom_call_target="tpu_custom_call" | custom-call | tf_op jit(solution)/shard_map/gradients/pallas_call | solution.py:492
  139.5 0.6 copy.13
  140.1 0.6 copy.14
  140.7 0.7 copy.15
Async XLA Ops:
  2.0 0.9 copy-start.2
  2.9 0.8 copy-start.3
  38.3 1.9 %copy-start = (bf16[1,1,96,128,128]{4,3,2,1,0:T(8,128)(2,1)S(1)}, bf16[1,1,96,128,128]{4,3,2,1,0:T(8,128)(2,1)}, u32[]{:S(2)}) copy-start(bf16[1,1,96,128,128]{4,3,2,1,0:T(8,128)(2,1)} %param.8) | copy-start | bytes 9437188
  40.2 3.2 %copy-start.5 = (bf16[128,256]{1,0:T(8,128)(2,1)S(1)}, bf16[128,256]{1,0:T(8,128)(2,1)}, u32[]{:S(2)}) copy-start(bf16[128,256]{1,0:T(8,128)(2,1)} %cotangent.1) | copy-start | bytes 196612
  40.2 39.0 %copy-start.1 = (bf16[1,1,96,128,128]{4,3,2,1,0:T(8,128)(2,1)S(1)}, bf16[1,1,96,128,128]{4,3,2,1,0:T(8,128)(2,1)}, u32[]{:S(2)}) copy-start(bf16[1,1,96,128,128]{4,3,2,1,0:T(8,128)(2,1)} %param.8) | copy-start | bytes 9437188
  79.3 3.2 %copy-start.4 = (bf16[128,256]{1,0:T(8,128)(2,1)S(1)}, bf16[128,256]{1,0:T(8,128)(2,1)}, u32[]{:S(2)}) copy-start(bf16[128,256]{1,0:T(8,128)(2,1)} %features.3) | copy-start | bytes 196612

commit v2 on v0

v2 whole, which is shorter than its diff:
```python
import jax
import jax.numpy as jnp
from jax import lax
from jax.experimental import pallas as pl
from jax.experimental.pallas import tpu as pltpu
from jax.sharding import PartitionSpec as P

F32 = jnp.float32
BF16 = jnp.bfloat16
MESH = pl.DeviceIdType.MESH
TILE = 128
HID = 256
TROWS = 32
TCOLS = 16
SLOTS = 96
VMEM_LIMIT = 58 * 2**20


def flip1(v):
    return v + 1 - 2 * lax.rem(v, 2)


def flip2(v):
    return lax.rem(v + 2, 4)


def flip3(v):
    return 3 - v


FLIPS = {0: lambda v: v, 1: flip1, 2: flip2, 3: flip3}


class Place:
    def __init__(self):
        row = lax.axis_index("row")
        col = lax.axis_index("col")
        self.y = lax.div(row, 4)
        self.zh = lax.rem(row, 4)
        self.zl = lax.div(col, 8)
        self.x = lax.rem(lax.div(col, 2), 4)
        self.core = lax.rem(col, 2)

    def peer(self, y=0, zh=0, zl=0, x=0, core=0):
        row = FLIPS[y](self.y) * 4 + FLIPS[zh](self.zh)
        col = FLIPS[zl](self.zl) * 8 + FLIPS[x](self.x) * 2 + FLIPS[core](self.core)
        return (row, col)


class Net:
    def __init__(self, send_sems, recv_sems):
        self.send_sems = send_sems
        self.recv_sems = recv_sems
        self.started = []

    def send(self, src, dst, device):
        i = len(self.started)
        copy = pltpu.make_async_remote_copy(
            src_ref=src,
            dst_ref=dst,
            send_sem=self.send_sems.at[i],
            recv_sem=self.recv_sems.at[i],
            device_id=device,
            device_id_type=MESH,
        )
        copy.start()
        self.started.append(copy)
        return copy

    def finish(self):
        for copy in self.started:
            copy.wait_send()


def greet(peers):
    barrier = pltpu.get_barrier_semaphore()
    for peer in peers:
        pl.semaphore_signal(barrier, inc=1, device_id=peer, device_id_type=MESH)
    pl.semaphore_wait(barrier, len(peers))


def add(*values):
    total = values[0].astype(F32)
    for value in values[1:]:
        total = total + value.astype(F32)
    return total.astype(BF16)


def ring_gather(net, at, near, far):
    copies = {}

    def first():
        copies["n0"] = net.send(at(0, 0), at(1, 0), near)
        copies["f1"] = net.send(at(0, 1), at(3, 1), far)
        copies["n1"] = net.send(at(0, 1), at(1, 1), near)
        copies["f0"] = net.send(at(0, 0), at(3, 0), far)

    def second():
        copies["n0"].wait_recv()
        copies["nf"] = net.send(at(1, 0), at(2, 0), far)
        copies["f1"].wait_recv()
        copies["fn"] = net.send(at(3, 1), at(2, 1), near)
        copies["n1"].wait_recv()
        copies["f0"].wait_recv()

    def third():
        copies["nf"].wait_recv()
        copies["fn"].wait_recv()

    return first, second, third


def ring_scatter(net, at, landing, near, far):
    copies = {}

    def first():
        copies["t1"] = net.send(at(2, 0), landing(2, 0), near)
        copies["t3"] = net.send(at(2, 1), landing(2, 1), far)
        copies["n0"] = net.send(at(1, 0), landing(0, 0), near)
        copies["f1"] = net.send(at(3, 1), landing(1, 1), far)

    def second():
        copies["t1"].wait_recv()
        share = at(3, 0)
        share[...] = add(share[...], landing(2, 0)[...])
        copies["f0"] = net.send(share, landing(1, 0), far)
        copies["t3"].wait_recv()
        share = at(1, 1)
        share[...] = add(share[...], landing(2, 1)[...])
        copies["n1"] = net.send(share, landing(0, 1), near)

    def third():
        for name in ("n0", "f1", "f0", "n1"):
            copies[name].wait_recv()

    return first, second, third


def halves(size):
    half = size // 2
    return {0: slice(0, half), 1: slice(half, size), None: slice(None)}


def kernel(
    slots, features, weight, tiles, cotangent,
    output, grad_features, grad_weight,
    held, feats, panel, mat, acc, partial, from_core, from_x, total_x, from_z,
    grads, back_acc, back, from_y, total_y, from_zh,
    cot, shares, got8, sum8, got4, got16, all4, all8,
    local_sems, send_sems, recv_sems,
):
    place = Place()
    net = Net(send_sems, recv_sems)
    node = halves(TILE)
    wide = halves(HID)

    load_feats = pltpu.make_async_copy(features, feats.at[0, 0], local_sems.at[0])
    load_weight = pltpu.make_async_copy(weight, mat, local_sems.at[1])
    load_tiles = pltpu.make_async_copy(tiles, held.at[pl.ds(0, SLOTS)], local_sems.at[2])
    load_cot = pltpu.make_async_copy(cotangent, cot, local_sems.at[3])
    for copy in (load_feats, load_weight, load_tiles, load_cot):
        copy.start()

    y_peers = {i: place.peer(y=i) for i in (1, 2, 3)}
    z_pairs = [(h, l) for h in range(4) for l in range(4) if h or l]
    z_peers = {pair: place.peer(zh=pair[0], zl=pair[1]) for pair in z_pairs}
    x_pairs = [(i, j) for i in range(4) for j in range(2) if i or j]
    x_peers = {pair: place.peer(x=pair[0], core=pair[1]) for pair in x_pairs}
    greet(tuple(y_peers.values()) + tuple(z_peers.values()) + tuple(x_peers.values()))
    zh_near, zh_far = z_peers[(1, 0)], z_peers[(3, 0)]
    y_near, y_far = y_peers[1], y_peers[3]
    x_near, x_far = x_peers[(1, 0)], x_peers[(3, 0)]
    other = x_peers[(0, 1)]
    along = {k: z_peers[(0, k)] for k in (1, 2, 3)}

    def at_zh(i, half):
        return feats.at[0, i, node[half]]

    def at_y(k):
        return lambda i, half: feats.at[i, k, node[half]]

    load_feats.wait()
    z_ring = ring_gather(net, at_zh, zh_near, zh_far)
    rings = {k: ring_gather(net, at_y(k), y_near, y_far) for k in (0, 1, 3)}
    z_ring[0]()
    rings[0][0]()
    held[SLOTS] = jnp.zeros((TILE, TILE), BF16)
    load_weight.wait()

    def project(k):
        def one(i, carry):
            panel[i, k] = jnp.dot(
                feats[i, k], mat[...], preferred_element_type=F32
            ).astype(BF16)
            return carry

        lax.fori_loop(0, 4, one, 0)

    def forward(targets, ks):
        places = [(i, k) for k in ks for i in range(4)]
        left = jnp.concatenate(
            [
                jnp.concatenate([held[slots[t * TCOLS + i * 4 + k]] for i, k in places], axis=1)
                for t in targets
            ],
            axis=0,
        )
        right = jnp.concatenate([panel[i, k] for i, k in places], axis=0)
        return jnp.dot(left, right, preferred_element_type=F32)

    def sweep(ks, first):
        def block(b, carry):
            targets = [b * 4 + i for i in range(4)]
            value = forward(targets, ks).reshape(4, TILE, HID)
            rows = pl.ds(b * 4, 4)
            acc[rows] = value if first else acc[rows] + value
            return carry

        lax.fori_loop(0, TROWS // 4, block, 0)

    rings[0][1]()
    z_ring[1]()
    rings[1][0]()
    rings[3][0]()
    rings[0][2]()
    load_tiles.wait()
    project(0)
    rings[1][1]()
    rings[3][1]()
    sweep((0,), True)
    z_ring[2]()
    direct = [net.send(feats.at[0, 2], feats.at[i, 2], y_peers[i]) for i in (1, 3, 2)]
    rings[1][2]()
    rings[3][2]()
    project(1)
    project(3)
    sweep((1, 3), False)
    for copy in direct:
        copy.wait_recv()
    project(2)

    order = (3, 2, 1, 0)

    def finish_block(k, core):
        targets = [k * 8 + x * 2 + core for x in range(4)]
        value = forward(targets, (2,))
        for x, t in enumerate(targets):
            rows = slice(x * TILE, (x + 1) * TILE)
            partial[k, x, core] = (acc[t] + value[rows]).astype(BF16)

    core_copies = {}
    for k in order:
        finish_block(k, 1)
        core_copies[k] = net.send(partial.at[k, :, 1], from_core.at[k], other)

    def at_x(k):
        return lambda i, half: from_core.at[k, i, node[half]]

    def land_x(k):
        return lambda i, half: from_x.at[k, i, node[half]]

    rings = {k: ring_scatter(net, at_x(k), land_x(k), x_near, x_far) for k in order}
    z_copies = {}

    def start(k):
        finish_block(k, 0)
        core_copies[k].wait_recv()
        for i in (2, 1, 3):
            from_core[k, i] = add(from_core[k, i], partial[k, i, 0])
        rings[k][0]()

    def close(k):
        rings[k][2]()
        parts = (partial[k, 0, 0], from_core[k, 0], from_x[k, 0], from_x[k, 1])
        if k:
            total_x[k] = add(*parts)
            z_copies[k] = net.send(total_x.at[k], from_z.at[k], along[k])
            return None
        return sum(part.astype(F32) for part in parts)

    start(3)
    start(2)
    start(1)
    rings[3][1]()
    start(0)
    rings[2][1]()
    close(3)
    rings[1][1]()
    close(2)
    rings[0][1]()
    close(1)
    hidden = close(0)
    load_cot.wait()
    for k in (3, 2, 1):
        z_copies[k].wait_recv()
        hidden = hidden + from_z[k].astype(F32)
    sig = jax.nn.sigmoid(hidden)
    slope = sig * (1.0 + hidden * (1.0 - sig))
    grads[0, 0, 0] = (cot[...].astype(F32) * slope).T.astype(BF16)

    out_copies = {k: net.send(grads.at[0, 0, 0], grads.at[k, 0, 0], along[k]) for k in (1, 2, 3)}

    def at_g(k):
        return lambda i, half: grads.at[k, i, 0, wide[half]]

    rounds = {k: ring_gather(net, at_g(k), x_near, x_far) for k in range(4)}
    rounds[0][0]()
    output[...] = (hidden * sig).astype(BF16)
    last = {}

    def swap(k):
        rounds[k][2]()
        last[k] = net.send(grads.at[k, :, 0], grads.at[k, :, 1], other)

    def backward(k, p):
        left = jnp.concatenate([grads[k, x, c] for x in range(4) for c in range(2)], axis=1)
        right = jnp.concatenate(
            [
                jnp.concatenate(
                    [held[slots[(k * 8 + j) * TCOLS + 2 * p + i]] for i in range(2)], axis=1
                )
                for j in range(8)
            ],
            axis=0,
        )
        return jnp.dot(left, right, preferred_element_type=F32)

    def back_sweep(k, first):
        last[k].wait_recv()

        def block(p, carry):
            value = backward(k, p)
            back_acc[p] = value if first else back_acc[p] + value
            return carry

        lax.fori_loop(0, TCOLS // 2, block, 0)

    out_copies[1].wait_recv()
    rounds[1][0]()
    rounds[0][1]()
    out_copies[2].wait_recv()
    rounds[2][0]()
    rounds[1][1]()
    swap(0)
    out_copies[3].wait_recv()
    rounds[3][0]()
    rounds[2][1]()
    swap(1)
    back_sweep(0, True)
    rounds[3][1]()
    swap(2)
    back_sweep(1, False)
    swap(3)
    back_sweep(2, False)
    last[3].wait_recv()

    def at_b(k):
        return lambda i, half: back.at[i, k, wide[half]]

    def land_y(k):
        return lambda i, half: from_y.at[k, i, wide[half]]

    rings = {k: ring_scatter(net, at_b(k), land_y(k), y_near, y_far) for k in range(4)}

    def back_pairs(pair):
        def block(i, carry):
            p = i * 2 + pair
            value = (back_acc[p] + backward(3, p)).astype(BF16)
            back[i, 2 * pair] = value[:, :TILE]
            back[i, 2 * pair + 1] = value[:, TILE:]
            return carry

        lax.fori_loop(0, 4, block, 0)

    back_pairs(1)
    rings[2][0]()
    rings[3][0]()
    back_pairs(0)
    rings[1][0]()

    chunks = [(i, k) for i in range(4) for k in range(4)]
    term = jnp.dot(
        jnp.concatenate([back[i, k] for i, k in chunks], axis=1),
        jnp.concatenate([feats[i, k] for i, k in chunks], axis=0),
        preferred_element_type=F32,
    ).astype(BF16)
    rings[0][0]()
    for p in range(8):
        for q in range(4):
            rows = p * 32 + (q // 2) * 16
            lanes = (q % 2) * 128
            shares[p, q] = term[rows:rows + 16, lanes:lanes + 128]
    me8 = place.x * 2 + place.core
    me16 = place.zh * 4 + place.zl
    copies8 = []
    for n, (i, j) in enumerate(x_pairs):
        there = FLIPS[i](place.x) * 2 + FLIPS[j](place.core)
        copies8.append(net.send(shares.at[there], got8.at[n], x_peers[(i, j)]))

    def close_y(k):
        rings[k][2]()
        total_y[k] = add(back[0, k], from_y[k, 0], from_y[k, 1])

    def zh_send(k, slot, half, peer):
        return net.send(total_y.at[k, wide[half]], from_zh.at[slot, wide[half]], peer)

    rings[2][1]()
    rings[3][1]()
    rings[1][1]()
    close_y(2)
    transit1 = zh_send(2, 2, 0, zh_near)
    transit3 = zh_send(2, 2, 1, zh_far)

    sum_own = shares[me8].astype(F32)
    for n, copy in enumerate(copies8):
        copy.wait_recv()
        sum_own = sum_own + got8[n].astype(F32)
    sum8[...] = sum_own.astype(BF16)
    copies4 = [
        net.send(sum8.at[FLIPS[i](place.y)], got4.at[i - 1], y_peers[i]) for i in (1, 2, 3)
    ]

    close_y(3)
    far1 = zh_send(3, 1, 1, zh_far)
    close_y(1)
    near0 = zh_send(1, 0, 0, zh_near)
    rings[0][1]()

    sum_own = sum8[place.y].astype(F32)
    for i, copy in enumerate(copies4):
        copy.wait_recv()
        sum_own = sum_own + got4[i].astype(F32)
    got16[me16] = sum_own.astype(BF16)
    copies16 = [net.send(got16.at[me16], got16.at[me16], z_peers[pair]) for pair in z_pairs]

    transit1.wait_recv()
    total_y[3, wide[0]] = add(total_y[3, wide[0]], from_zh[2, wide[0]])
    far0 = zh_send(3, 1, 0, zh_far)
    transit3.wait_recv()
    total_y[1, wide[1]] = add(total_y[1, wide[1]], from_zh[2, wide[1]])
    near1 = zh_send(1, 0, 1, zh_near)
    rings[0][2]()
    own = back[0, 0].astype(F32) + from_y[0, 0].astype(F32) + from_y[0, 1].astype(F32)

    for copy in copies16:
        copy.wait_recv()
    sum_all = got16[0].astype(F32)
    for n in range(1, 16):
        sum_all = sum_all + got16[n].astype(F32)
    all4[place.y] = sum_all.astype(BF16)
    copies4 = [net.send(all4.at[place.y], all4.at[place.y], y_peers[i]) for i in (1, 2, 3)]

    for copy in (near0, far1, far0, near1):
        copy.wait_recv()
    own = own + from_zh[0].astype(F32) + from_zh[1].astype(F32)
    grad_features[...] = lax.dot_general(
        own.T.astype(BF16), mat[...], (((1,), (1,)), ((), ())), preferred_element_type=F32
    ).astype(BF16)

    for copy in copies4:
        copy.wait_recv()
    copies8 = [net.send(all4, all8.at[me8], x_peers[pair]) for pair in x_pairs]
    all8[me8] = all4[...]
    for copy in copies8:
        copy.wait_recv()
    for p in range(8):
        for q in range(4):
            rows = p * 32 + (q // 2) * 16
            lanes = (q % 2) * 128
            grad_weight[rows:rows + 16, lanes:lanes + 128] = all8[p, q].astype(F32)
    net.finish()


VM = pl.BlockSpec(memory_space=pltpu.VMEM)
SM = pl.BlockSpec(memory_space=pltpu.SMEM)
ANY = pl.BlockSpec(memory_space=pl.ANY)
LINKS = 160


def shape(*dims, dtype=BF16):
    return jax.ShapeDtypeStruct(dims, dtype)


def buf(*dims, dtype=BF16):
    return pltpu.VMEM(dims, dtype)


def body(features, weight, tiles, coords, counts, cotangent):
    my_coords = coords[0, 0]
    code = (my_coords[:, 0] ^ lax.axis_index("col")) * TCOLS + (
        my_coords[:, 1] ^ lax.axis_index("row")
    )
    slot = jnp.arange(SLOTS, dtype=jnp.int32)
    code = jnp.where(slot < counts[0, 0], code, -1)
    place = jnp.arange(TROWS * TCOLS, dtype=jnp.int32)
    hit = code[:, None] == place[None, :]
    slots = SLOTS + jnp.sum(jnp.where(hit, slot[:, None] - SLOTS, 0), axis=0, dtype=jnp.int32)

    output, grad_features, grad_weight = pl.pallas_call(
        kernel,
        out_shape=(shape(TILE, HID), shape(TILE, HID), shape(HID, HID, dtype=F32)),
        in_specs=[SM, ANY, ANY, ANY, ANY],
        out_specs=(VM, VM, VM),
        scratch_shapes=[
            buf(SLOTS + 1, TILE, TILE),
            buf(4, 4, TILE, HID),
            buf(4, 4, TILE, HID),
            buf(HID, HID),
            buf(TROWS, TILE, HID, dtype=F32),
            buf(4, 4, 2, TILE, HID),
            buf(4, 4, TILE, HID),
            buf(4, 3, TILE, HID),
            buf(4, TILE, HID),
            buf(4, TILE, HID),
            buf(4, 4, 2, HID, TILE),
            buf(TCOLS // 2, HID, HID, dtype=F32),
            buf(4, 4, HID, TILE),
            buf(4, 3, HID, TILE),
            buf(4, HID, TILE),
            buf(3, HID, TILE),
            buf(TILE, HID),
            buf(8, 4, 16, 128),
            buf(7, 4, 16, 128),
            buf(4, 16, 128),
            buf(3, 16, 128),
            buf(16, 16, 128),
            buf(4, 16, 128),
            buf(8, 4, 16, 128),
            pltpu.SemaphoreType.DMA((4,)),
            pltpu.SemaphoreType.DMA((LINKS,)),
            pltpu.SemaphoreType.DMA((LINKS,)),
        ],
        compiler_params=pltpu.CompilerParams(
            collective_id=1, has_side_effects=True, vmem_limit_bytes=VMEM_LIMIT
        ),
        name="layer",
    )(slots, features, weight, tiles[0, 0], cotangent)
    return output, grad_features, grad_weight.T


def solution(mesh):
    placed = (
        P(("col", "row"), None),
        P(),
        P("row", "col", None, None, None),
        P("row", "col", None, None),
        P("row", "col"),
        P(("row", "col"), None),
    )
    return jax.shard_map(
        body,
        mesh=mesh,
        in_specs=placed,
        out_specs=(P(("row", "col"), None), P(("col", "row"), None), P()),
        check_vma=False,
    )
```

time: 1010 us -> 121 us (0.12)
  waiting for transfers between devices: 879 us -> 0 us
  Pallas kernels: 0 us -> 111 us
  matrix products: 73 us -> 0 us
  local copies, waits for them, and re-layouts: 34.4 us -> 4.73 us
  between operations: 13.8 us -> 1.29 us
    psum x1 -> x0, waiting for transfers between devices: 455 us -> none  [body(): grad_weight = lax.psum(weight_term, ('row', 'col'))]
    reduce_scatter x2 -> x0, waiting for transfers between devices: 259 us -> none  [the longest x1 133 us: body(): lax.psum_scatter(partial_sum.reshape(tile_rows * tile_size, width), 'col'...]
    all_gather x2 -> x0, waiting for transfers between devices: 164 us -> none  [the longest x1 84.9 us: body(): gathered = lax.all_gather(features, 'row', axis=0, tiled=True)]
    pallas_call x0 -> x1, Pallas kernels: none -> 111 us  [body(): pl.pallas_call(kernel, out_shape=(shape(TILE, HID), shape(TILE, HID), sha...]
    dot_general x27 -> x0, matrix products: 73 us -> none  [the longest x12 49.8 us: add_block(): return total + jnp.einsum('sr,sih->rih', onehot, prod)]
    gather x12 -> x0, local copies, waits for them, and re-layouts: 16.9 us -> none  [add_block(): picked = source[block_coords[:, which_source]]]
    while x2 -> x0, local copies, waits for them, and re-layouts: 10.8 us -> none  [tile_products(): return lax.fori_loop(0, block_total, add_block, start)]
  transfers between devices with their start and end apart: 5 -> 0, of which waited for: 5 -> 0; matrix products, arithmetic and copies ran while one was open for 0% -> 0% of each run, Pallas kernels for 0% -> 0%
where the time goes in v2:
time: 121 us; the launch traced here: 118 us
  Pallas kernels  111 us (92%)
  local copies, waits for them, and re-layouts  4.73 us (4%)
  other arithmetic  1.46 us (1%)
  between operations  1.29 us (1%)
    pallas_call x1, Pallas kernels, body(): pl.pallas_call(kernel, out_shape=(shape(TILE, HID), shape(TILE, HID), sha...  111 us
    unnamed x3, local copies, waits for them, and re-layouts  4.73 us

profile of v2, /device:TPU:6, one launch (start us, length us, event | category | flops | bytes accessed | tf_op | source)
XLA Modules:
  0.0 118.1 jit_solution(12300561323608159574)
XLA Ops:
  1.3 0.8 fusion
  2.0 0.1 select_reduce_fusion
  2.2 0.6 broadcast_add_fusion.slots
  2.7 110.6 %layer.1 = (bf16[128,256]{1,0:T(8,128)(2,1)}, bf16[128,256]{1,0:T(8,128)(2,1)}, f32[256,256]{1,0:T(8,128)}) custom-call(s32[512]{0:T(512)} %broadcast_add_fusion.slots, bf16[128,256]{1,0:T(8,128)(2,1)} %features.1, bf16[256,256]{1,0:T(8,128)(2,1)} %weight.1, bf16[96,128,128]{2,1,0:T(8,128)(2,1)} %bitcast.7, bf16[128,256]{1,0:T(8,128)(2,1)} %cotangent.1), custom_call_target="tpu_custom_call" | custom-call | tf_op jit(solution)/shard_map/layer/pallas_call | solution.py:499
  113.4 1.8 %copy.10 = f32[256,256]{1,0:T(8,128)} copy(f32[256,256]{0,1:T(8,128)} %bitcast.8) | data formatting | bytes 524288
  115.2 1.5 %copy.14 = bf16[128,256]{1,0:T(8,128)(2,1)} copy(bf16[128,256]{1,0:T(8,128)(2,1)} %get-tuple-element.18) | data formatting | bytes 131072
  116.7 1.5 %copy.15 = bf16[128,256]{1,0:T(8,128)(2,1)} copy(bf16[128,256]{1,0:T(8,128)(2,1)} %get-tuple-element.19) | data formatting | bytes 131072
  (1 shorter events, 0.0 us)

commit v3 on v2

--- a/solution.py
+++ b/solution.py
@@ -76,7 +76,7 @@
     barrier = pltpu.get_barrier_semaphore()
     for peer in peers:
         pl.semaphore_signal(barrier, inc=1, device_id=peer, device_id_type=MESH)
-    pl.semaphore_wait(barrier, len(peers))
+    return lambda: pl.semaphore_wait(barrier, len(peers))
 
 
 def add(*values):
@@ -107,6 +107,7 @@
         copies["nf"].wait_recv()
         copies["fn"].wait_recv()
 
+    third.halves = (lambda: copies["nf"].wait_recv(), lambda: copies["fn"].wait_recv())
     return first, second, third
 
 
@@ -142,11 +143,11 @@
 
 
 def kernel(
-    slots, features, weight, tiles, cotangent,
+    coords, count, features, weight, tiles, cotangent,
     output, grad_features, grad_weight,
-    held, feats, panel, mat, acc, partial, from_core, from_x, total_x, from_z,
-    grads, back_acc, back, from_y, total_y, from_zh,
-    cot, shares, got8, sum8, got4, got16, all4, all8,
+    held, feats, mat, acc, partial, from_core, from_x, total_x, from_z,
+    grads, back_acc, back, from_y, direct_y, total_y, from_zh,
+    cot, shares, got8, sum8, got4, got16, all4, all8, spots, places, slots,
     local_sems, send_sems, recv_sems,
 ):
     place = Place()
@@ -154,19 +155,19 @@
     node = halves(TILE)
     wide = halves(HID)
 
-    load_feats = pltpu.make_async_copy(features, feats.at[0, 0], local_sems.at[0])
-    load_weight = pltpu.make_async_copy(weight, mat, local_sems.at[1])
-    load_tiles = pltpu.make_async_copy(tiles, held.at[pl.ds(0, SLOTS)], local_sems.at[2])
-    load_cot = pltpu.make_async_copy(cotangent, cot, local_sems.at[3])
-    for copy in (load_feats, load_weight, load_tiles, load_cot):
-        copy.start()
-
     y_peers = {i: place.peer(y=i) for i in (1, 2, 3)}
     z_pairs = [(h, l) for h in range(4) for l in range(4) if h or l]
     z_peers = {pair: place.peer(zh=pair[0], zl=pair[1]) for pair in z_pairs}
     x_pairs = [(i, j) for i in range(4) for j in range(2) if i or j]
     x_peers = {pair: place.peer(x=pair[0], core=pair[1]) for pair in x_pairs}
-    greet(tuple(y_peers.values()) + tuple(z_peers.values()) + tuple(x_peers.values()))
+    arrived = greet(tuple(y_peers.values()) + tuple(z_peers.values()) + tuple(x_peers.values()))
+    load_feats = pltpu.make_async_copy(features, feats.at[0, 0], local_sems.at[0])
+    load_weight = pltpu.make_async_copy(weight, mat, local_sems.at[1])
+    load_tiles = pltpu.make_async_copy(tiles, held.at[pl.ds(0, SLOTS)], local_sems.at[2])
+    load_cot = pltpu.make_async_copy(cotangent, cot, local_sems.at[3])
+    for copy in (load_feats, load_tiles, load_weight, load_cot):
+        copy.start()
+
     zh_near, zh_far = z_peers[(1, 0)], z_peers[(3, 0)]
     y_near, y_far = y_peers[1], y_peers[3]
     x_near, x_far = x_peers[(1, 0)], x_peers[(3, 0)]
@@ -180,32 +181,36 @@
         return lambda i, half: feats.at[i, k, node[half]]
 
     load_feats.wait()
+    arrived()
     z_ring = ring_gather(net, at_zh, zh_near, zh_far)
     rings = {k: ring_gather(net, at_y(k), y_near, y_far) for k in (0, 1, 3)}
     z_ring[0]()
     rings[0][0]()
+
+    spots[...] = jnp.zeros((8, 128), jnp.int32)
+    spots[0:2, 0:SLOTS] = coords[...]
+    far_row = jnp.broadcast_to(spots[0:1, :], (128, 128)).T[:SLOTS] ^ lax.axis_index("col")
+    far_col = jnp.broadcast_to(spots[1:2, :], (128, 128)).T[:SLOTS] ^ lax.axis_index("row")
+    slot = lax.broadcasted_iota(jnp.int32, (SLOTS, 128), 0)
+    lane = lax.broadcasted_iota(jnp.int32, (SLOTS, 128), 1)
+    value = jnp.where((far_col == lane) & (slot < count[0, 0]), slot - SLOTS, 0)
+    for t in range(TROWS):
+        found = jnp.where(far_row == t, value, 0)
+        places[t:t + 1] = SLOTS + jnp.sum(found, axis=0, keepdims=True)
+    load_slots = pltpu.make_async_copy(places, slots, local_sems.at[4])
+    load_slots.start()
     held[SLOTS] = jnp.zeros((TILE, TILE), BF16)
-    load_weight.wait()
-
-    def project(k):
-        def one(i, carry):
-            panel[i, k] = jnp.dot(
-                feats[i, k], mat[...], preferred_element_type=F32
-            ).astype(BF16)
-            return carry
-
-        lax.fori_loop(0, 4, one, 0)
 
     def forward(targets, ks):
         places = [(i, k) for k in ks for i in range(4)]
         left = jnp.concatenate(
             [
-                jnp.concatenate([held[slots[t * TCOLS + i * 4 + k]] for i, k in places], axis=1)
+                jnp.concatenate([held[slots[t, i * 4 + k]] for i, k in places], axis=1)
                 for t in targets
             ],
             axis=0,
         )
-        right = jnp.concatenate([panel[i, k] for i, k in places], axis=0)
+        right = jnp.concatenate([feats[i, k] for i, k in places], axis=0)
         return jnp.dot(left, right, preferred_element_type=F32)
 
     def sweep(ks, first):
@@ -218,26 +223,26 @@
 
         lax.fori_loop(0, TROWS // 4, block, 0)
 
-    rings[0][1]()
     z_ring[1]()
     rings[1][0]()
     rings[3][0]()
+    rings[0][1]()
     rings[0][2]()
     load_tiles.wait()
-    project(0)
+    load_slots.wait()
+    sweep((0,), True)
     rings[1][1]()
     rings[3][1]()
-    sweep((0,), True)
-    z_ring[2]()
-    direct = [net.send(feats.at[0, 2], feats.at[i, 2], y_peers[i]) for i in (1, 3, 2)]
+    direct = []
+    for wait, half in zip(z_ring[2].halves, (0, 1)):
+        wait()
+        for i in (2, 1, 3):
+            direct.append(net.send(at_zh(2, half), at_y(2)(i, half), y_peers[i]))
     rings[1][2]()
     rings[3][2]()
-    project(1)
-    project(3)
     sweep((1, 3), False)
     for copy in direct:
         copy.wait_recv()
-    project(2)
 
     order = (3, 2, 1, 0)
 
@@ -289,11 +294,14 @@
     close(2)
     rings[0][1]()
     close(1)
-    hidden = close(0)
+    own = close(0)
     load_cot.wait()
+    load_weight.wait()
     for k in (3, 2, 1):
         z_copies[k].wait_recv()
-        hidden = hidden + from_z[k].astype(F32)
+        own = own + from_z[k].astype(F32)
+    summed = own.astype(BF16)
+    hidden = jnp.dot(summed, mat[...], preferred_element_type=F32)
     sig = jax.nn.sigmoid(hidden)
     slope = sig * (1.0 + hidden * (1.0 - sig))
     grads[0, 0, 0] = (cot[...].astype(F32) * slope).T.astype(BF16)
@@ -305,8 +313,72 @@
 
     rounds = {k: ring_gather(net, at_g(k), x_near, x_far) for k in range(4)}
     rounds[0][0]()
-    output[...] = (hidden * sig).astype(BF16)
     last = {}
+
+    def unpacked(p, q):
+        rows = p * 32 + (q // 2) * 16
+        lanes = (q % 2) * 128
+        return slice(rows, rows + 16), slice(lanes, lanes + 128)
+
+    me8 = place.x * 2 + place.core
+    me16 = place.zh * 4 + place.zl
+    sums = {}
+
+    def sum_start():
+        term = jnp.dot(grads[0, 0, 0], summed, preferred_element_type=F32).astype(BF16)
+        for p in range(8):
+            for q in range(4):
+                rows, lanes = unpacked(p, q)
+                shares[p, q] = term[rows, lanes]
+        sums[0] = [
+            net.send(
+                shares.at[FLIPS[i](place.x) * 2 + FLIPS[j](place.core)],
+                got8.at[n], x_peers[(i, j)],
+            )
+            for n, (i, j) in enumerate(x_pairs)
+        ]
+
+    def sum_8():
+        total = shares[me8].astype(F32)
+        for n, copy in enumerate(sums[0]):
+            copy.wait_recv()
+            total = total + got8[n].astype(F32)
+        sum8[...] = total.astype(BF16)
+        sums[1] = [
+            net.send(sum8.at[FLIPS[i](place.y)], got4.at[i - 1], y_peers[i]) for i in (1, 2, 3)
+        ]
+
+    def sum_4():
+        total = sum8[place.y].astype(F32)
+        for i, copy in enumerate(sums[1]):
+            copy.wait_recv()
+            total = total + got4[i].astype(F32)
+        got16[me16] = total.astype(BF16)
+        sums[2] = [net.send(got16.at[me16], got16.at[me16], z_peers[pair]) for pair in z_pairs]
+
+    def sum_16():
+        for copy in sums[2]:
+            copy.wait_recv()
+        total = got16[0].astype(F32)
+        for n in range(1, 16):
+            total = total + got16[n].astype(F32)
+        all4[place.y] = total.astype(BF16)
+        sums[3] = [net.send(all4.at[place.y], all4.at[place.y], y_peers[i]) for i in (1, 2, 3)]
+
+    def spread_4():
+        for copy in sums[3]:
+            copy.wait_recv()
+        sums[4] = [net.send(all4, all8.at[me8], x_peers[pair]) for pair in x_pairs]
+        all8[me8] = all4[...]
+
+    def sum_end():
+        for copy in sums[4]:
+            copy.wait_recv()
+        rows = [
+            jnp.concatenate([all8[p, q].astype(F32), all8[p, q + 1].astype(F32)], axis=1)
+            for p in range(8) for q in (0, 2)
+        ]
+        grad_weight[...] = jnp.concatenate(rows, axis=0).T
 
     def swap(k):
         rounds[k][2]()
@@ -317,7 +389,7 @@
         right = jnp.concatenate(
             [
                 jnp.concatenate(
-                    [held[slots[(k * 8 + j) * TCOLS + 2 * p + i]] for i in range(2)], axis=1
+                    [held[slots[k * 8 + j, 2 * p + i]] for i in range(2)], axis=1
                 )
                 for j in range(8)
             ],
@@ -335,17 +407,21 @@
 
         lax.fori_loop(0, TCOLS // 2, block, 0)
 
+    sum_start()
     out_copies[1].wait_recv()
     rounds[1][0]()
     rounds[0][1]()
+    output[...] = (hidden * sig).astype(BF16)
     out_copies[2].wait_recv()
     rounds[2][0]()
+    sum_8()
     rounds[1][1]()
     swap(0)
     out_copies[3].wait_recv()
     rounds[3][0]()
     rounds[2][1]()
     swap(1)
+    sum_4()
     back_sweep(0, True)
     rounds[3][1]()
     swap(2)
@@ -360,7 +436,7 @@
     def land_y(k):
         return lambda i, half: from_y.at[k, i, wide[half]]
 
-    rings = {k: ring_scatter(net, at_b(k), land_y(k), y_near, y_far) for k in range(4)}
+    rings = {k: ring_scatter(net, at_b(k), land_y(k), y_near, y_far) for k in (0, 1, 3)}
 
     def back_pairs(pair):
         def block(i, carry):
@@ -372,108 +448,67 @@
 
         lax.fori_loop(0, 4, block, 0)
 
+    def zh_send(k, slot, half, peer):
+        return net.send(total_y.at[k, wide[half]], from_zh.at[slot, wide[half]], peer)
+
+    def close_y(k):
+        rings[k][2]()
+        total_y[k] = add(back[0, k], from_y[k, 0], from_y[k, 1])
+
     back_pairs(1)
-    rings[2][0]()
+    direct = {
+        half: [net.send(at_b(2)(i, half), direct_y.at[i - 1, wide[half]], y_peers[i]) for i in (2, 1, 3)]
+        for half in (0, 1)
+    }
     rings[3][0]()
     back_pairs(0)
     rings[1][0]()
-
-    chunks = [(i, k) for i in range(4) for k in range(4)]
-    term = jnp.dot(
-        jnp.concatenate([back[i, k] for i, k in chunks], axis=1),
-        jnp.concatenate([feats[i, k] for i, k in chunks], axis=0),
-        preferred_element_type=F32,
-    ).astype(BF16)
     rings[0][0]()
-    for p in range(8):
-        for q in range(4):
-            rows = p * 32 + (q // 2) * 16
-            lanes = (q % 2) * 128
-            shares[p, q] = term[rows:rows + 16, lanes:lanes + 128]
-    me8 = place.x * 2 + place.core
-    me16 = place.zh * 4 + place.zl
-    copies8 = []
-    for n, (i, j) in enumerate(x_pairs):
-        there = FLIPS[i](place.x) * 2 + FLIPS[j](place.core)
-        copies8.append(net.send(shares.at[there], got8.at[n], x_peers[(i, j)]))
-
-    def close_y(k):
-        rings[k][2]()
-        total_y[k] = add(back[0, k], from_y[k, 0], from_y[k, 1])
-
-    def zh_send(k, slot, half, peer):
-        return net.send(total_y.at[k, wide[half]], from_zh.at[slot, wide[half]], peer)
-
-    rings[2][1]()
+    sum_16()
+    transit = {}
+    for half, peer in ((0, zh_near), (1, zh_far)):
+        for copy in direct[half]:
+            copy.wait_recv()
+        rows = wide[half]
+        total_y[2, rows] = add(
+            back[0, 2, rows], direct_y[0, rows], direct_y[1, rows], direct_y[2, rows]
+        )
+        transit[half] = zh_send(2, 2, half, peer)
     rings[3][1]()
     rings[1][1]()
-    close_y(2)
-    transit1 = zh_send(2, 2, 0, zh_near)
-    transit3 = zh_send(2, 2, 1, zh_far)
-
-    sum_own = shares[me8].astype(F32)
-    for n, copy in enumerate(copies8):
-        copy.wait_recv()
-        sum_own = sum_own + got8[n].astype(F32)
-    sum8[...] = sum_own.astype(BF16)
-    copies4 = [
-        net.send(sum8.at[FLIPS[i](place.y)], got4.at[i - 1], y_peers[i]) for i in (1, 2, 3)
-    ]
-
+    rings[0][1]()
     close_y(3)
     far1 = zh_send(3, 1, 1, zh_far)
     close_y(1)
     near0 = zh_send(1, 0, 0, zh_near)
-    rings[0][1]()
-
-    sum_own = sum8[place.y].astype(F32)
-    for i, copy in enumerate(copies4):
-        copy.wait_recv()
-        sum_own = sum_own + got4[i].astype(F32)
-    got16[me16] = sum_own.astype(BF16)
-    copies16 = [net.send(got16.at[me16], got16.at[me16], z_peers[pair]) for pair in z_pairs]
-
-    transit1.wait_recv()
+    spread_4()
+    transit[0].wait_recv()
     total_y[3, wide[0]] = add(total_y[3, wide[0]], from_zh[2, wide[0]])
     far0 = zh_send(3, 1, 0, zh_far)
-    transit3.wait_recv()
+    transit[1].wait_recv()
     total_y[1, wide[1]] = add(total_y[1, wide[1]], from_zh[2, wide[1]])
     near1 = zh_send(1, 0, 1, zh_near)
     rings[0][2]()
     own = back[0, 0].astype(F32) + from_y[0, 0].astype(F32) + from_y[0, 1].astype(F32)
-
-    for copy in copies16:
-        copy.wait_recv()
-    sum_all = got16[0].astype(F32)
-    for n in range(1, 16):
-        sum_all = sum_all + got16[n].astype(F32)
-    all4[place.y] = sum_all.astype(BF16)
-    copies4 = [net.send(all4.at[place.y], all4.at[place.y], y_peers[i]) for i in (1, 2, 3)]
-
+    sum_end()
     for copy in (near0, far1, far0, near1):
         copy.wait_recv()
     own = own + from_zh[0].astype(F32) + from_zh[1].astype(F32)
     grad_features[...] = lax.dot_general(
         own.T.astype(BF16), mat[...], (((1,), (1,)), ((), ())), preferred_element_type=F32
     ).astype(BF16)
-
-    for copy in copies4:
-        copy.wait_recv()
-    copies8 = [net.send(all4, all8.at[me8], x_peers[pair]) for pair in x_pairs]
-    all8[me8] = all4[...]
-    for copy in copies8:
-        copy.wait_recv()
-    for p in range(8):
-        for q in range(4):
-            rows = p * 32 + (q // 2) * 16
-            lanes = (q % 2) * 128
-            grad_weight[rows:rows + 16, lanes:lanes + 128] = all8[p, q].astype(F32)
     net.finish()
+
+
+def hand_over(out_in, grad_in, weight_in, output, grad_features, grad_weight):
+    output[...] = out_in[...]
+    grad_features[...] = grad_in[...]
+    grad_weight[...] = weight_in[...]
 
 
 VM = pl.BlockSpec(memory_space=pltpu.VMEM)
 SM = pl.BlockSpec(memory_space=pltpu.SMEM)
-ANY = pl.BlockSpec(memory_space=pl.ANY)
+HBM = pl.BlockSpec(memory_space=pltpu.HBM)
 LINKS = 160
 
 
@@ -486,24 +521,14 @@
 
 
 def body(features, weight, tiles, coords, counts, cotangent):
-    my_coords = coords[0, 0]
-    code = (my_coords[:, 0] ^ lax.axis_index("col")) * TCOLS + (
-        my_coords[:, 1] ^ lax.axis_index("row")
-    )
-    slot = jnp.arange(SLOTS, dtype=jnp.int32)
-    code = jnp.where(slot < counts[0, 0], code, -1)
-    place = jnp.arange(TROWS * TCOLS, dtype=jnp.int32)
-    hit = code[:, None] == place[None, :]
-    slots = SLOTS + jnp.sum(jnp.where(hit, slot[:, None] - SLOTS, 0), axis=0, dtype=jnp.int32)
-
-    output, grad_features, grad_weight = pl.pallas_call(
+    shapes = (shape(TILE, HID), shape(TILE, HID), shape(HID, HID, dtype=F32))
+    results = pl.pallas_call(
         kernel,
-        out_shape=(shape(TILE, HID), shape(TILE, HID), shape(HID, HID, dtype=F32)),
-        in_specs=[SM, ANY, ANY, ANY, ANY],
+        out_shape=shapes,
+        in_specs=[VM, SM, HBM, HBM, HBM, HBM],
         out_specs=(VM, VM, VM),
         scratch_shapes=[
             buf(SLOTS + 1, TILE, TILE),
-            buf(4, 4, TILE, HID),
             buf(4, 4, TILE, HID),
             buf(HID, HID),
             buf(TROWS, TILE, HID, dtype=F32),
@@ -516,6 +541,7 @@
             buf(TCOLS // 2, HID, HID, dtype=F32),
             buf(4, 4, HID, TILE),
             buf(4, 3, HID, TILE),
+            buf(3, HID, TILE),
             buf(4, HID, TILE),
             buf(3, HID, TILE),
             buf(TILE, HID),
@@ -526,7 +552,10 @@
             buf(16, 16, 128),
             buf(4, 16, 128),
             buf(8, 4, 16, 128),
-            pltpu.SemaphoreType.DMA((4,)),
+            buf(8, 128, dtype=jnp.int32),
+            buf(TROWS, 128, dtype=jnp.int32),
+            pltpu.SMEM((TROWS, 128), jnp.int32),
+            pltpu.SemaphoreType.DMA((5,)),
             pltpu.SemaphoreType.DMA((LINKS,)),
             pltpu.SemaphoreType.DMA((LINKS,)),
         ],
@@ -534,8 +563,14 @@
             collective_id=1, has_side_effects=True, vmem_limit_bytes=VMEM_LIMIT
         ),
         name="layer",
-    )(slots, features, weight, tiles[0, 0], cotangent)
-    return output, grad_features, grad_weight.T
+    )(coords[0, 0].T, counts, features, weight, tiles[0, 0], cotangent)
+    return pl.pallas_call(
+        hand_over,
+        out_shape=shapes,
+        in_specs=[VM] * 3,
+        out_specs=(VM,) * 3,
+        name="hand_over",
+    )(*results)
 
 
 def solution(mesh):

time: 121 us -> 105 us (0.87)
  Pallas kernels: 111 us -> 102 us
  local copies, waits for them, and re-layouts: 4.73 us -> 0 us
  other arithmetic: 1.46 us -> 0 us
    pallas_call x1 -> x2, Pallas kernels: 111 us -> 102 us  [the longest x1 100 us: body(): pl.pallas_call(kernel, out_shape=shapes, in_specs=[VM, SM, HBM, HBM, HBM,...]
    unnamed x3 -> x0, local copies, waits for them, and re-layouts: 4.73 us -> none
where the time goes in v3:
time: 105 us; the launch traced here: 103 us
  Pallas kernels  102 us (97%)
  between operations  1.29 us (1%)
    pallas_call x1, Pallas kernels, body(): pl.pallas_call(kernel, out_shape=shapes, in_specs=[VM, SM, HBM, HBM, HBM,...  100 us

profile of v3, /device:TPU:6, one launch (start us, length us, event | category | flops | bytes accessed | tf_op | source)
XLA Modules:
  0.0 103.1 jit_solution(9736289485321860651)
XLA Ops:
  1.3 100.0 %layer.1 = (bf16[128,256]{1,0:T(8,128)(2,1)}, bf16[128,256]{1,0:T(8,128)(2,1)}, f32[256,256]{1,0:T(8,128)}) custom-call(s32[2,96]{1,0:T(2,128)} %bitcast.5, s32[1,1]{1,0:T(1,128)S(6)} %copy.9.count, bf16[128,256]{1,0:T(8,128)(2,1)} %features.1, bf16[256,256]{1,0:T(8,128)(2,1)} %weight.1, bf16[96,128,128]{2,1,0:T(8,128)(2,1)} %bitcast.4, ...), custom_call_target="tpu_custom_call" | custom-call | tf_op jit(solution)/shard_map/layer/pallas_call | solution.py:525
  101.3 1.8 %hand_over.1 = (bf16[128,256]{1,0:T(8,128)(2,1)}, bf16[128,256]{1,0:T(8,128)(2,1)}, f32[256,256]{1,0:T(8,128)}) custom-call(bf16[128,256]{1,0:T(8,128)(2,1)} %get-tuple-element.6.out_in, bf16[128,256]{1,0:T(8,128)(2,1)} %get-tuple-element.7.grad_in, f32[256,256]{1,0:T(8,128)} %get-tuple-element.8.weight_in), custom_call_target="tpu_custom_call" | custom-call | tf_op jit(solution)/shard_map/hand_over/pallas_call | solution.py:567

commit v4 on v3

--- a/solution.py
+++ b/solution.py
@@ -52,6 +52,7 @@
         self.send_sems = send_sems
         self.recv_sems = recv_sems
         self.started = []
+        self.finished = 0
 
     def send(self, src, dst, device):
         i = len(self.started)
@@ -68,8 +69,9 @@
         return copy
 
     def finish(self):
-        for copy in self.started:
+        for copy in self.started[self.finished:]:
             copy.wait_send()
+        self.finished = len(self.started)
 
 
 def greet(peers):
@@ -86,12 +88,16 @@
     return total.astype(BF16)
 
 
-def ring_gather(net, at, near, far):
+def ring_gather(net, at, near, far, late=False):
     copies = {}
 
     def first():
         copies["n0"] = net.send(at(0, 0), at(1, 0), near)
         copies["f1"] = net.send(at(0, 1), at(3, 1), far)
+        if not late:
+            rest()
+
+    def rest():
         copies["n1"] = net.send(at(0, 1), at(1, 1), near)
         copies["f0"] = net.send(at(0, 0), at(3, 0), far)
 
@@ -107,6 +113,7 @@
         copies["nf"].wait_recv()
         copies["fn"].wait_recv()
 
+    first.rest = rest
     third.halves = (lambda: copies["nf"].wait_recv(), lambda: copies["fn"].wait_recv())
     return first, second, third
 
@@ -147,7 +154,7 @@
     output, grad_features, grad_weight,
     held, feats, mat, acc, partial, from_core, from_x, total_x, from_z,
     grads, back_acc, back, from_y, direct_y, total_y, from_zh,
-    cot, shares, got8, sum8, got4, got16, all4, all8, spots, places, slots,
+    cot, shares, got8, sum8, got16, pair, all4, all8, activated, summed_weight, spots, places, slots,
     local_sems, send_sems, recv_sems,
 ):
     place = Place()
@@ -156,23 +163,26 @@
     wide = halves(HID)
 
     y_peers = {i: place.peer(y=i) for i in (1, 2, 3)}
-    z_pairs = [(h, l) for h in range(4) for l in range(4) if h or l]
-    z_peers = {pair: place.peer(zh=pair[0], zl=pair[1]) for pair in z_pairs}
+    z_peers = {i: place.peer(zh=i) for i in (1, 3)}
+    along = {i: place.peer(zl=i) for i in (1, 2, 3)}
+    yz_pairs = [(i, j) for i in range(4) for j in range(4) if i or j]
+    yz_peers = {pair: place.peer(y=pair[0], zl=pair[1]) for pair in yz_pairs}
     x_pairs = [(i, j) for i in range(4) for j in range(2) if i or j]
     x_peers = {pair: place.peer(x=pair[0], core=pair[1]) for pair in x_pairs}
-    arrived = greet(tuple(y_peers.values()) + tuple(z_peers.values()) + tuple(x_peers.values()))
     load_feats = pltpu.make_async_copy(features, feats.at[0, 0], local_sems.at[0])
+    load_feats.start()
+    partners = [*z_peers.values(), *yz_peers.values(), *x_peers.values()]
+    arrived = greet(partners)
     load_weight = pltpu.make_async_copy(weight, mat, local_sems.at[1])
     load_tiles = pltpu.make_async_copy(tiles, held.at[pl.ds(0, SLOTS)], local_sems.at[2])
     load_cot = pltpu.make_async_copy(cotangent, cot, local_sems.at[3])
-    for copy in (load_feats, load_tiles, load_weight, load_cot):
+    for copy in (load_tiles, load_weight, load_cot):
         copy.start()
 
-    zh_near, zh_far = z_peers[(1, 0)], z_peers[(3, 0)]
+    zh_near, zh_far = z_peers[1], z_peers[3]
     y_near, y_far = y_peers[1], y_peers[3]
     x_near, x_far = x_peers[(1, 0)], x_peers[(3, 0)]
     other = x_peers[(0, 1)]
-    along = {k: z_peers[(0, k)] for k in (1, 2, 3)}
 
     def at_zh(i, half):
         return feats.at[0, i, node[half]]
@@ -182,7 +192,7 @@
 
     load_feats.wait()
     arrived()
-    z_ring = ring_gather(net, at_zh, zh_near, zh_far)
+    z_ring = ring_gather(net, at_zh, zh_near, zh_far, late=True)
     rings = {k: ring_gather(net, at_y(k), y_near, y_far) for k in (0, 1, 3)}
     z_ring[0]()
     rings[0][0]()
@@ -199,6 +209,7 @@
         places[t:t + 1] = SLOTS + jnp.sum(found, axis=0, keepdims=True)
     load_slots = pltpu.make_async_copy(places, slots, local_sems.at[4])
     load_slots.start()
+    z_ring[0].rest()
     held[SLOTS] = jnp.zeros((TILE, TILE), BF16)
 
     def forward(targets, ks):
@@ -254,7 +265,8 @@
             partial[k, x, core] = (acc[t] + value[rows]).astype(BF16)
 
     core_copies = {}
-    for k in order:
+
+    def give_core(k):
         finish_block(k, 1)
         core_copies[k] = net.send(partial.at[k, :, 1], from_core.at[k], other)
 
@@ -268,7 +280,6 @@
     z_copies = {}
 
     def start(k):
-        finish_block(k, 0)
         core_copies[k].wait_recv()
         for i in (2, 1, 3):
             from_core[k, i] = add(from_core[k, i], partial[k, i, 0])
@@ -283,12 +294,20 @@
             return None
         return sum(part.astype(F32) for part in parts)
 
+    give_core(3)
+    finish_block(3, 0)
+    give_core(2)
     start(3)
+    finish_block(2, 0)
+    give_core(1)
     start(2)
+    finish_block(1, 0)
+    rings[3][1]()
+    give_core(0)
     start(1)
-    rings[3][1]()
+    finish_block(0, 0)
+    rings[2][1]()
     start(0)
-    rings[2][1]()
     close(3)
     rings[1][1]()
     close(2)
@@ -321,8 +340,8 @@
         return slice(rows, rows + 16), slice(lanes, lanes + 128)
 
     me8 = place.x * 2 + place.core
-    me16 = place.zh * 4 + place.zl
     sums = {}
+    save_weight = pltpu.make_async_copy(summed_weight, grad_weight, local_sems.at[6])
 
     def sum_start():
         term = jnp.dot(grads[0, 0, 0], summed, preferred_element_type=F32).astype(BF16)
@@ -344,41 +363,45 @@
             copy.wait_recv()
             total = total + got8[n].astype(F32)
         sum8[...] = total.astype(BF16)
+        got16[place.y, place.zl] = sum8[place.y]
         sums[1] = [
-            net.send(sum8.at[FLIPS[i](place.y)], got4.at[i - 1], y_peers[i]) for i in (1, 2, 3)
+            net.send(
+                sum8.at[FLIPS[i](place.y)], got16.at[place.y, place.zl], yz_peers[(i, j)]
+            )
+            for i, j in yz_pairs
         ]
 
-    def sum_4():
-        total = sum8[place.y].astype(F32)
-        for i, copy in enumerate(sums[1]):
+    def sum_16():
+        for copy in sums[1]:
             copy.wait_recv()
-            total = total + got4[i].astype(F32)
-        got16[me16] = total.astype(BF16)
-        sums[2] = [net.send(got16.at[me16], got16.at[me16], z_peers[pair]) for pair in z_pairs]
-
-    def sum_16():
-        for copy in sums[2]:
+        pair[0] = add(*(got16[i, j] for i in range(4) for j in range(4)))
+        sums[3] = net.send(pair.at[0], pair.at[1], zh_near)
+
+    def sum_near():
+        sums[3].wait_recv()
+        pair[2] = add(pair[0], pair[1])
+        sums[4] = net.send(pair.at[2], pair.at[3], zh_far)
+
+    def sum_far():
+        sums[4].wait_recv()
+        all4[place.y] = add(pair[2], pair[3])
+        sums[5] = [net.send(all4.at[place.y], all4.at[place.y], y_peers[i]) for i in (1, 2, 3)]
+
+    def spread_4():
+        for copy in sums[5]:
             copy.wait_recv()
-        total = got16[0].astype(F32)
-        for n in range(1, 16):
-            total = total + got16[n].astype(F32)
-        all4[place.y] = total.astype(BF16)
-        sums[3] = [net.send(all4.at[place.y], all4.at[place.y], y_peers[i]) for i in (1, 2, 3)]
-
-    def spread_4():
-        for copy in sums[3]:
-            copy.wait_recv()
-        sums[4] = [net.send(all4, all8.at[me8], x_peers[pair]) for pair in x_pairs]
+        sums[6] = [net.send(all4, all8.at[me8], x_peers[pair]) for pair in x_pairs]
         all8[me8] = all4[...]
 
     def sum_end():
-        for copy in sums[4]:
+        for copy in sums[6]:
             copy.wait_recv()
         rows = [
             jnp.concatenate([all8[p, q].astype(F32), all8[p, q + 1].astype(F32)], axis=1)
             for p in range(8) for q in (0, 2)
         ]
-        grad_weight[...] = jnp.concatenate(rows, axis=0).T
+        summed_weight[...] = jnp.concatenate(rows, axis=0).T
+        save_weight.start()
 
     def swap(k):
         rounds[k][2]()
@@ -411,7 +434,9 @@
     out_copies[1].wait_recv()
     rounds[1][0]()
     rounds[0][1]()
-    output[...] = (hidden * sig).astype(BF16)
+    activated[...] = (hidden * sig).astype(BF16)
+    save_output = pltpu.make_async_copy(activated, output, local_sems.at[5])
+    save_output.start()
     out_copies[2].wait_recv()
     rounds[2][0]()
     sum_8()
@@ -421,13 +446,14 @@
     rounds[3][0]()
     rounds[2][1]()
     swap(1)
-    sum_4()
     back_sweep(0, True)
     rounds[3][1]()
+    sum_16()
     swap(2)
     back_sweep(1, False)
     swap(3)
     back_sweep(2, False)
+    sum_near()
     last[3].wait_recv()
 
     def at_b(k):
@@ -464,7 +490,6 @@
     back_pairs(0)
     rings[1][0]()
     rings[0][0]()
-    sum_16()
     transit = {}
     for half, peer in ((0, zh_near), (1, zh_far)):
         for copy in direct[half]:
@@ -477,20 +502,22 @@
     rings[3][1]()
     rings[1][1]()
     rings[0][1]()
+    sum_far()
     close_y(3)
     far1 = zh_send(3, 1, 1, zh_far)
     close_y(1)
     near0 = zh_send(1, 0, 0, zh_near)
-    spread_4()
     transit[0].wait_recv()
     total_y[3, wide[0]] = add(total_y[3, wide[0]], from_zh[2, wide[0]])
     far0 = zh_send(3, 1, 0, zh_far)
+    spread_4()
     transit[1].wait_recv()
     total_y[1, wide[1]] = add(total_y[1, wide[1]], from_zh[2, wide[1]])
     near1 = zh_send(1, 0, 1, zh_near)
     rings[0][2]()
     own = back[0, 0].astype(F32) + from_y[0, 0].astype(F32) + from_y[0, 1].astype(F32)
     sum_end()
+    net.finish()
     for copy in (near0, far1, far0, near1):
         copy.wait_recv()
     own = own + from_zh[0].astype(F32) + from_zh[1].astype(F32)
@@ -498,6 +525,8 @@
         own.T.astype(BF16), mat[...], (((1,), (1,)), ((), ())), preferred_element_type=F32
     ).astype(BF16)
     net.finish()
+    save_output.wait()
+    save_weight.wait()
 
 
 def hand_over(out_in, grad_in, weight_in, output, grad_features, grad_weight):
@@ -526,7 +555,7 @@
         kernel,
         out_shape=shapes,
         in_specs=[VM, SM, HBM, HBM, HBM, HBM],
-        out_specs=(VM, VM, VM),
+        out_specs=(HBM, VM, HBM),
         scratch_shapes=[
             buf(SLOTS + 1, TILE, TILE),
             buf(4, 4, TILE, HID),
@@ -548,14 +577,16 @@
             buf(8, 4, 16, 128),
             buf(7, 4, 16, 128),
             buf(4, 16, 128),
-            buf(3, 16, 128),
-            buf(16, 16, 128),
+            buf(4, 4, 16, 128),
+            buf(4, 16, 128),
             buf(4, 16, 128),
             buf(8, 4, 16, 128),
+            buf(TILE, HID),
+            buf(HID, HID, dtype=F32),
             buf(8, 128, dtype=jnp.int32),
             buf(TROWS, 128, dtype=jnp.int32),
             pltpu.SMEM((TROWS, 128), jnp.int32),
-            pltpu.SemaphoreType.DMA((5,)),
+            pltpu.SemaphoreType.DMA((7,)),
             pltpu.SemaphoreType.DMA((LINKS,)),
             pltpu.SemaphoreType.DMA((LINKS,)),
         ],

time: 105 us -> 103 us (0.981)
  Pallas kernels: 102 us -> 100 us
    pallas_call x1, Pallas kernels: 100 us -> 98.6 us  [body(): pl.pallas_call(kernel, out_shape=shapes, in_specs=[VM, SM, HBM, HBM, HBM,...]
where the time goes in v4:
time: 103 us; the launch traced here: 102 us
  Pallas kernels  100 us (97%)
  between operations  1.29 us (1%)
    pallas_call x1, Pallas kernels, body(): pl.pallas_call(kernel, out_shape=shapes, in_specs=[VM, SM, HBM, HBM, HBM,...  98.6 us

profile of v4, /device:TPU:6, one launch (start us, length us, event | category | flops | bytes accessed | tf_op | source)
XLA Modules:
  0.0 101.6 jit_solution(21295660259007834)
XLA Ops:
  1.3 98.6 %layer.1 = (bf16[128,256]{1,0:T(8,128)(2,1)}, bf16[128,256]{1,0:T(8,128)(2,1)}, f32[256,256]{1,0:T(8,128)}) custom-call(s32[2,96]{1,0:T(2,128)} %bitcast.5, s32[1,1]{1,0:T(1,128)S(6)} %copy.9.count, bf16[128,256]{1,0:T(8,128)(2,1)} %features.1, bf16[256,256]{1,0:T(8,128)(2,1)} %weight.1, bf16[96,128,128]{2,1,0:T(8,128)(2,1)} %bitcast.4, ...), custom_call_target="tpu_custom_call" | custom-call | tf_op jit(solution)/shard_map/layer/pallas_call | solution.py:554
  99.9 1.8 %hand_over.1 = (bf16[128,256]{1,0:T(8,128)(2,1)}, bf16[128,256]{1,0:T(8,128)(2,1)}, f32[256,256]{1,0:T(8,128)}) custom-call(bf16[128,256]{1,0:T(8,128)(2,1)} %get-tuple-element.6.out_in, bf16[128,256]{1,0:T(8,128)(2,1)} %get-tuple-element.7.grad_in, f32[256,256]{1,0:T(8,128)} %get-tuple-element.8.weight_in), custom_call_target="tpu_custom_call" | custom-call | tf_op jit(solution)/shard_map/hand_over/pallas_call | solution.py:598

commit v5 on v4

--- a/solution.py
+++ b/solution.py
@@ -481,12 +481,21 @@
         rings[k][2]()
         total_y[k] = add(back[0, k], from_y[k, 0], from_y[k, 1])
 
-    back_pairs(1)
-    direct = {
-        half: [net.send(at_b(2)(i, half), direct_y.at[i - 1, wide[half]], y_peers[i]) for i in (2, 1, 3)]
-        for half in (0, 1)
-    }
+    def back_pair(i, pair_of):
+        p = i * 2 + pair_of
+        value = (back_acc[p] + backward(3, p)).astype(BF16)
+        back[i, 2 * pair_of] = value[:, :TILE]
+        back[i, 2 * pair_of + 1] = value[:, TILE:]
+
+    direct = {0: [], 1: []}
+    for i in (2, 1, 3):
+        back_pair(i, 1)
+        for half in (0, 1):
+            direct[half].append(
+                net.send(at_b(2)(i, half), direct_y.at[i - 1, wide[half]], y_peers[i])
+            )
     rings[3][0]()
+    back_pair(0, 1)
     back_pairs(0)
     rings[1][0]()
     rings[0][0]()

time: 103 us -> 103 us (level)
  no operation moved by 1% of the time
where the time goes in v5:
time: 103 us; the launch traced here: 101 us
  Pallas kernels  99.6 us (97%)
  between operations  1.29 us (1%)
    pallas_call x1, Pallas kernels, body(): pl.pallas_call(kernel, out_shape=shapes, in_specs=[VM, SM, HBM, HBM, HBM,...  97.8 us

profile of v5, /device:TPU:6, one launch (start us, length us, event | category | flops | bytes accessed | tf_op | source)
XLA Modules:
  0.0 100.9 jit_solution(17932892825507932398)
XLA Ops:
  1.3 97.8 %layer.1 = (bf16[128,256]{1,0:T(8,128)(2,1)}, bf16[128,256]{1,0:T(8,128)(2,1)}, f32[256,256]{1,0:T(8,128)}) custom-call(s32[2,96]{1,0:T(2,128)} %bitcast.5, s32[1,1]{1,0:T(1,128)S(6)} %copy.9.count, bf16[128,256]{1,0:T(8,128)(2,1)} %features.1, bf16[256,256]{1,0:T(8,128)(2,1)} %weight.1, bf16[96,128,128]{2,1,0:T(8,128)(2,1)} %bitcast.4, ...), custom_call_target="tpu_custom_call" | custom-call | tf_op jit(solution)/shard_map/layer/pallas_call | solution.py:563
  99.1 1.8 %hand_over.1 = (bf16[128,256]{1,0:T(8,128)(2,1)}, bf16[128,256]{1,0:T(8,128)(2,1)}, f32[256,256]{1,0:T(8,128)}) custom-call(bf16[128,256]{1,0:T(8,128)(2,1)} %get-tuple-element.6.out_in, bf16[128,256]{1,0:T(8,128)(2,1)} %get-tuple-element.7.grad_in, f32[256,256]{1,0:T(8,128)} %get-tuple-element.8.weight_in), custom_call_target="tpu_custom_call" | custom-call | tf_op jit(solution)/shard_map/hand_over/pallas_call | solution.py:607
